TPU v7x, 256 devices: a whole 4x4x8 slice. The times are simulated.
256 devices in a mesh: dp: 16 (over z_hi, y), space: 16 (over z_lo, x, core).
Axes of the slice: x: 4, y: 4, z: 8 (z_hi: 4, z_lo: 2; z = z_hi * 2 + z_lo), core: 2. Of those that a mesh axis runs over, the one named last changes fastest.
Arguments:
- queries_raw: bfloat16 [16, 6144, 2560], P('dp', 'space'), as said below
- keys_raw: bfloat16 [16, 6144, 2560], P('dp', 'space'), as said below
- values: bfloat16 [16, 6144, 2560], P('dp', 'space'), may hold values from -6 to 6
- out_grad: bfloat16 [16, 6144, 2560], P('dp', 'space'), may hold values from -288 to 288
- q_gain: float32 [2560], replicated, may hold values from 0.1 to 1.9
- k_gain: float32 [2560], replicated, may hold values from 0.1 to 1.9
Outputs:
- key_grad: bfloat16 [16, 6144, 2560], P('dp', 'space')
- value_grad: bfloat16 [16, 6144, 2560], P('dp', 'space')
- q_gain_grad: float32 [2560], replicated
- k_gain_grad: float32 [2560], replicated
Inputs may be any that keep to these rules, and one draw needn't show every extreme that they name: `queries_raw`: Real-valued projections. `keys_raw`: Real-valued projections.
All inputs are finite; a program needn't handle non-finite values.
Results may differ from a plain program's by a relative error of at most 0.012.
The roundings to bfloat16 on the way count: a program that leaves them out, or rounds other values in their place, can miss the bound.
Values may be sent and summed in bfloat16 or wider, within the bound.
A program may use at most 128 MiB of HBM per device.

v0:
```python
import jax
import jax.numpy as jnp
from jax import lax
from jax.sharding import PartitionSpec as P

HS = 128
R = 192


epsilon = 1e-06
group_heads = 4


def from_behind(block, axis, distance):
    devices = range(lax.axis_size(axis))
    route = [(i - distance, i) for i in devices if i - distance in devices]
    return lax.ppermute(block, axis, route)


def normalize(raw):
    wide = raw.astype(jnp.float32)
    inverse = lax.rsqrt(jnp.mean(wide * wide, axis=-1, keepdims=True) + epsilon)
    return (wide * inverse, inverse)


def split_heads(block_data):
    return block_data.reshape(block_data.shape[:-1] + (group_heads, HS))


def key_side(dscores, probs_b, query3, grad3):
    scale = HS ** (-0.5)
    count = dscores.shape[2]
    dkey = jnp.einsum("hqk,qhd->khd", dscores, query3, preferred_element_type=jnp.float32) * scale
    dvalue = jnp.einsum("hqk,qhd->khd", probs_b, grad3, preferred_element_type=jnp.float32)
    return (dkey.reshape(count, -1), dvalue.reshape(count, -1))


def attend(query, keys, values, grad_out):
    scale = HS ** (-0.5)
    query4 = split_heads(query)
    keys4 = split_heads(keys)
    values4 = split_heads(values)
    grad4 = split_heads(grad_out)
    scores = (
        jnp.einsum("tqhd,tkhd->thqk", query4, keys4, preferred_element_type=jnp.float32) * scale
    )
    row_top = jnp.max(scores, axis=-1, keepdims=True)
    expo = jnp.exp(scores - row_top)
    row_total = jnp.sum(expo, axis=-1, keepdims=True)
    probs = expo / row_total
    probs_b = probs.astype(jnp.bfloat16)
    attended = jnp.einsum("thqk,tkhd->tqhd", probs_b, values4, preferred_element_type=jnp.float32)
    row_delta = jnp.swapaxes(jnp.sum(grad4.astype(jnp.float32) * attended, axis=-1), 1, 2)
    dprobs = jnp.einsum("tqhd,tkhd->thqk", grad4, values4, preferred_element_type=jnp.float32)
    dscores = (probs * (dprobs - row_delta[..., None])).astype(jnp.bfloat16)
    dquery = (
        jnp.einsum("thqk,tkhd->tqhd", dscores, keys4, preferred_element_type=jnp.float32) * scale
    )
    return (
        dquery.reshape(query.shape),
        dscores,
        probs_b,
        row_top[..., 0],
        row_total[..., 0],
        row_delta,
        query4,
        grad4,
    )


def per_device(queries_raw, keys_raw, values, out_grad, q_gain, k_gain):
    num_rows = queries_raw.shape[1]
    num_features = queries_raw.shape[2]
    pair_count = lax.axis_size("space")
    pair_index = lax.axis_index("space")
    tile_count = 2 * pair_count
    head_count = num_features // HS
    group_width = group_heads * HS
    group_count = num_features // group_width
    qn, q_inverse = normalize(queries_raw[0])
    kn, k_inverse = normalize(keys_raw[0])
    query = (qn * q_gain).astype(jnp.bfloat16)
    key = (kn * k_gain).astype(jnp.bfloat16)
    value = values[0]
    grad_out = out_grad[0]
    fetched = []
    for shift_by, row_begin in ((1, R), (-1, 0)):
        fetched.append(
            from_behind(
                (key[row_begin : row_begin + R], value[row_begin : row_begin + R]),
                "space",
                shift_by,
            )
        )
    near_keys = jnp.concatenate([fetched[0][0], key, fetched[1][0]], axis=0)
    near_values = jnp.concatenate([fetched[0][1], value, fetched[1][1]], axis=0)
    offsets = [
        jnp.clip(2 * pair_index + which_tile, 1, tile_count - 2) - 2 * pair_index
        for which_tile in (0, 1)
    ]
    window_keys = jnp.stack(
        [
            lax.dynamic_slice_in_dim(near_keys, offsets[which_tile] * R, 3 * R, 0)
            for which_tile in (0, 1)
        ]
    )
    window_values = jnp.stack(
        [
            lax.dynamic_slice_in_dim(near_values, offsets[which_tile] * R, 3 * R, 0)
            for which_tile in (0, 1)
        ]
    )
    query_pair = query.reshape(2, R, num_features)
    grad_pair = grad_out.reshape(2, R, num_features)
    key_rows = 4 * R

    def reader_step(group_index, state_now):
        dquery_all, dkey_all, dvalue_all, top_all, total_all, delta_all = state_now
        column = group_index * group_width

        def columns(array):
            return lax.dynamic_slice_in_dim(array, column, group_width, 2)

        dquery, dscores, probs_b, row_top, row_total, row_delta, query4, grad4 = attend(
            columns(query_pair), columns(window_keys), columns(window_values), columns(grad_pair)
        )
        group_key = jnp.zeros((key_rows, group_width), jnp.float32)
        group_value = jnp.zeros((key_rows, group_width), jnp.float32)
        for which_tile in (0, 1):
            dkey, dvalue = key_side(
                dscores[which_tile], probs_b[which_tile], query4[which_tile], grad4[which_tile]
            )
            row_begin = offsets[which_tile] * R
            group_key = lax.dynamic_update_slice_in_dim(
                group_key,
                lax.dynamic_slice_in_dim(group_key, row_begin, 3 * R, 0) + dkey,
                row_begin,
                0,
            )
            group_value = lax.dynamic_update_slice_in_dim(
                group_value,
                lax.dynamic_slice_in_dim(group_value, row_begin, 3 * R, 0) + dvalue,
                row_begin,
                0,
            )
        head_begin = group_index * group_heads
        dquery_all = lax.dynamic_update_slice_in_dim(
            dquery_all, dquery.reshape(num_rows, group_width), column, 1
        )
        dkey_all = lax.dynamic_update_slice_in_dim(dkey_all, group_key, column, 1)
        dvalue_all = lax.dynamic_update_slice_in_dim(dvalue_all, group_value, column, 1)
        top_all = lax.dynamic_update_slice_in_dim(top_all, row_top, head_begin, 1)
        total_all = lax.dynamic_update_slice_in_dim(total_all, row_total, head_begin, 1)
        delta_all = lax.dynamic_update_slice_in_dim(delta_all, row_delta, head_begin, 1)
        return (dquery_all, dkey_all, dvalue_all, top_all, total_all, delta_all)

    start_state = (
        jnp.zeros((num_rows, num_features), jnp.float32),
        jnp.zeros((key_rows, num_features), jnp.float32),
        jnp.zeros((key_rows, num_features), jnp.float32),
        jnp.zeros((2, head_count, R), jnp.float32),
        jnp.zeros((2, head_count, R), jnp.float32),
        jnp.zeros((2, head_count, R), jnp.float32),
    )
    dquery_all, dkey_all, dvalue_all, top_all, total_all, delta_all = lax.fori_loop(
        0, group_count, reader_step, start_state
    )
    key_total = dkey_all[R : 3 * R]
    value_total = dvalue_all[R : 3 * R]
    for shift_by, row_begin, target in ((-1, 0, R), (1, 3 * R, 0)):
        got_key, got_value = from_behind(
            (
                dkey_all[row_begin : row_begin + R].astype(jnp.bfloat16),
                dvalue_all[row_begin : row_begin + R].astype(jnp.bfloat16),
            ),
            "space",
            shift_by,
        )
        key_total = lax.dynamic_update_slice_in_dim(
            key_total, key_total[target : target + R] + got_key.astype(jnp.float32), target, 0
        )
        value_total = lax.dynamic_update_slice_in_dim(
            value_total, value_total[target : target + R] + got_value.astype(jnp.float32), target, 0
        )
    dkn = key_total * k_gain
    key_grad = (k_inverse * (dkn - kn * jnp.mean(dkn * kn, axis=-1, keepdims=True))).astype(
        jnp.bfloat16
    )
    value_grad = value_total.astype(jnp.bfloat16)
    q_part = jnp.sum(dquery_all * qn, axis=0)
    k_part = jnp.sum(key_total * kn, axis=0)
    q_sum, k_sum = lax.psum((q_part, k_part), ("dp", "space"))
    factor = (lax.axis_size("dp") * lax.axis_size("space") * num_rows) ** (-0.5)
    return (key_grad[None], value_grad[None], q_sum * factor, k_sum * factor)


def solution(mesh):
    return jax.shard_map(
        per_device,
        mesh=mesh,
        in_specs=(
            P("dp", "space", None),
            P("dp", "space", None),
            P("dp", "space", None),
            P("dp", "space", None),
            P(),
            P(),
        ),
        out_specs=(P("dp", "space", None), P("dp", "space", None), P(), P()),
        check_vma=False,
    )
```

profile of v0, /device:TPU:1, one launch (start us, length us, event | category | flops | bytes accessed | tf_op | source)
XLA Modules:
  0.0 297.5 jit_solution(3888049461189394949)
XLA Ops:
  0.6 2.0 fusion.41
  2.7 2.2 fusion.35
  4.9 1.4 fusion.51
  6.3 4.6 %collective-permute-start = (bf16[192,2560]{1,0:T(8,128)(2,1)}, bf16[192,2560]{1,0:T(8,128)(2,1)}, u32[]{:S(2)}, u32[]{:S(2)}) collective-permute-start(bf16[192,2560]{1,0:T(8,128)(2,1)} %get-tuple-element.292), channel_id=1, source_target_pairs={{0,1},{1,2},{2,3},{3,4},{4,5},{5,6},{6,7},{7,8},{8,9},{9,10},{10,1... | collective-permute-start | bytes 2949128 | tf_op jit(solution)/shard_map/ppermute | solution.py:17
  11.0 2.9 collective-permute-start.1
  13.9 1.4 slice_bitcast_fusion.9
  15.3 2.7 collective-permute-start.2
  18.0 2.6 collective-permute-start.3
  21.1 2.2 multiply_convert_fusion.1
  23.4 3.3 %collective-permute-done.1 = bf16[192,2560]{1,0:T(8,128)(2,1)} collective-permute-done((bf16[192,2560]{1,0:T(8,128)(2,1)}, bf16[192,2560]{1,0:T(8,128)(2,1)}, u32[]{:S(2)}, u32[]{:S(2)}) %collective-permute-start.1) | collective-permute-done | bytes 983072 | tf_op jit(solution)/shard_map/ppermute | solution.py:17
  26.7 3.3 %pad_maximum_fusion.2 = bf16[768,2560]{1,0:T(8,128)(2,1)} fusion(bf16[192,2560]{1,0:T(8,128)(2,1)} %collective-permute-done.1, bf16[384,2560]{1,0:T(8,128)(2,1)S(1)} %copy-done.5, bf16[192,2560]{1,0:T(8,128)(2,1)} %collective-permute-done), kind=kLoop, calls=%fused_computation.73 | loop fusion | flops 11796480 | bytes 7864320 | tf_op jit(solution)/shard_map/concatenate | solution.py:95
  30.0 2.9 collective-permute-done.2
  32.8 4.4 %collective-permute-done.3 = bf16[192,2560]{1,0:T(8,128)(2,1)} collective-permute-done((bf16[192,2560]{1,0:T(8,128)(2,1)}, bf16[192,2560]{1,0:T(8,128)(2,1)}, u32[]{:S(2)}, u32[]{:S(2)}) %collective-permute-start.3) | collective-permute-done | bytes 983072 | tf_op jit(solution)/shard_map/ppermute | solution.py:17
  37.2 3.3 %pad_maximum_fusion.3 = bf16[768,2560]{1,0:T(8,128)(2,1)} fusion(bf16[192,2560]{1,0:T(8,128)(2,1)} %collective-permute-done.3, bf16[384,2560]{1,0:T(8,128)(2,1)S(1)} %bitcast.195, bf16[192,2560]{1,0:T(8,128)(2,1)} %collective-permute-done.2), kind=kLoop, calls=%fused_computation.74 | loop fusion | flops 11796480 | bytes 7864320 | tf_op jit(solution)/shard_map/concatenate | solution.py:96
  40.5 9.1 %dynamic-slice_bitcast_fusion.5 = (bf16[1,576,2560]{2,1,0:T(8,128)(2,1)}, bf16[1,576,2560]{2,1,0:T(8,128)(2,1)}, bf16[1,576,2560]{2,1,0:T(8,128)(2,1)}, bf16[1,576,2560]{2,1,0:T(8,128)(2,1)}) fusion(bf16[768,2560]{1,0:T(8,128)(2,1)} %pad_maximum_fusion.3, s32[]{:T(128)} %select_n.41, s32[]{:T(128)} %select_n.42, bf16[768,2560]{1,0:T(8,128)(2,1)} %pad_maximum_fusion.2), kind=kLoop, calls=%fused_computation.82 | loop fusion | bytes 23592968 | tf_op jit(solution)/shard_map/stack | solution.py:107
  49.6 5.9 %pad_maximum_fusion.1 = bf16[2,576,2560]{2,1,0:T(8,128)(2,1)} fusion(bf16[1,576,2560]{2,1,0:T(8,128)(2,1)} %get-tuple-element.287, bf16[1,576,2560]{2,1,0:T(8,128)(2,1)} %get-tuple-element.286), kind=kLoop, calls=%fused_computation.59 | loop fusion | flops 2949120 | bytes 11796480 | tf_op jit(solution)/shard_map/stack | solution.py:107
  55.5 3.1 %pad_maximum_fusion = bf16[2,576,2560]{2,1,0:T(8,128)(2,1)} fusion(bf16[1,576,2560]{2,1,0:T(8,128)(2,1)S(1)} %copy-done.7, bf16[1,576,2560]{2,1,0:T(8,128)(2,1)S(1)} %copy-done.8), kind=kLoop, calls=%fused_computation.58 | loop fusion | flops 2949120 | bytes 11796480 | tf_op jit(solution)/shard_map/stack | solution.py:101
  58.6 2.5 broadcast_in_dim.24
  61.1 4.1 %broadcast.100.clone = f32[768,2560]{1,0:T(8,128)} broadcast(f32[]{:T(128)} %constant.99.clone.1), dimensions={} | broadcast | bytes 7864324 | tf_op jit(solution)/shard_map/broadcast.13
  65.2 4.0 %broadcast.100 = f32[768,2560]{1,0:T(8,128)} broadcast(f32[]{:T(128)} %constant.99.clone.1), dimensions={} | broadcast | bytes 7864324 | tf_op jit(solution)/shard_map/broadcast.13
  69.2 99.0 %while.19 = (s32[]{:T(128)}, f32[384,2560]{1,0:T(8,128)}, f32[768,2560]{1,0:T(8,128)}, f32[768,2560]{1,0:T(8,128)}, bf16[2,576,2560]{2,1,0:T(8,128)(2,1)}, /*ind...) while((s32[]{:T(128)}, f32[384,2560]{1,0:T(8,128)}, ...), condition=%wide.region_6.7_spmd, body=%wide.region_2.6_spmd.sunk | while | flops 1369766912 | bytes 68453632 | solution.py:165
  70.5 2.0 fusion.86
  72.5 2.0 fusion.87
  74.9 2.1 fusion.89
  77.0 2.2 multiply_convert_fusion.3
  79.2 1.9 fusion.90
  90.3 2.0 fusion.86
  92.3 2.0 fusion.87
  94.6 2.1 fusion.89
  96.8 2.2 multiply_convert_fusion.3
  98.9 1.9 fusion.90
  106.0 1.4 constant_dynamic-update-slice_fusion.4
  107.4 1.4 constant_dynamic-update-slice_fusion.5
  110.1 2.0 fusion.86
  112.1 2.0 fusion.87
  114.5 2.1 fusion.89
  116.6 2.2 multiply_convert_fusion.3
  118.8 1.9 fusion.90
  125.9 1.4 constant_dynamic-update-slice_fusion.4
  129.9 2.0 fusion.86
  131.9 2.0 fusion.87
  134.2 2.1 fusion.89
  136.4 2.2 multiply_convert_fusion.3
  138.5 1.9 fusion.90
  147.0 1.4 constant_dynamic-update-slice_fusion.5
  149.7 2.0 fusion.86
  151.7 2.0 fusion.87
  154.1 2.1 fusion.89
  156.2 2.2 multiply_convert_fusion.3
  158.4 2.0 fusion.90
  165.5 1.4 constant_dynamic-update-slice_fusion.4
  168.2 3.8 %convert.12 = bf16[768,2560]{1,0:T(8,128)(2,1)S(1)} convert(f32[768,2560]{1,0:T(8,128)} %get-tuple-element.248) | non-fusion elementwise | flops 1966080 | bytes 11796480 | tf_op jit(solution)/shard_map/convert.4
  172.1 1.4 fusion.49
  173.5 2.4 collective-permute-start.7
  175.9 2.5 collective-permute-start.6
  179.0 1.5 copy-done.6
  182.7 3.1 %collective-permute-start.5 = (bf16[192,2560]{1,0:T(8,128)(2,1)S(1)}, bf16[192,2560]{1,0:T(8,128)(2,1)S(1)}, u32[]{:S(2)}, u32[]{:S(2)}) collective-permute-start(bf16[192,2560]{1,0:T(8,128)(2,1)S(1)} %get-tuple-element.284), channel_id=1, source_target_pairs={{0,1},{1,2},{2,3},{3,4},{4,5},{5,6},{6,7},{7,8},{8,9},{9,10},{10,1... | collective-permute-start | bytes 2949128 | tf_op jit(solution)/shard_map/ppermute | solution.py:17
  185.8 1.9 collective-permute-start.4
  187.8 3.8 %collective-permute-done.6 = bf16[192,2560]{1,0:T(8,128)(2,1)S(1)} collective-permute-done((bf16[192,2560]{1,0:T(8,128)(2,1)}, bf16[192,2560]{1,0:T(8,128)(2,1)S(1)}, u32[]{:S(2)}, u32[]{:S(2)}) %collective-permute-start.6) | collective-permute-done | bytes 983072 | tf_op jit(solution)/shard_map/ppermute | solution.py:17
  192.2 9.9 %collective-permute-done.4 = bf16[192,2560]{1,0:T(8,128)(2,1)S(1)} collective-permute-done((bf16[192,2560]{1,0:T(8,128)(2,1)S(1)}, bf16[192,2560]{1,0:T(8,128)(2,1)S(1)}, u32[]{:S(2)}, u32[]{:S(2)}) %collective-permute-start.4) | collective-permute-done | bytes 983072 | tf_op jit(solution)/shard_map/ppermute | solution.py:17
  202.3 1.5 convert_bitcast_fusion
  204.2 1.8 copy-done
  207.2 84.7 %all-reduce = (f32[2560]{0:T(1024)S(1)}, f32[2560]{0:T(1024)S(1)}) all-reduce(f32[2560]{0:T(1024)S(1)} %fusion.44, f32[2560]{0:T(1024)S(1)} %get-tuple-element.250), channel_id=1, replica_groups=mesh['dp'=16,'space'=16] {'dp','space'}, use_global_device_ids=true, to_apply=%region_9.10 | all-reduce | flops 5120 | bytes 40960 | tf_op jit(solution)/shard_map/psum | solution.py:192
  292.5 4.4 %fusion.45 = bf16[1,384,2560]{2,1,0:T(8,128)(2,1)} fusion(f32[384,2560]{1,0:T(8,128)} %copy-done, bf16[1,384,2560]{2,1,0:T(8,128)(2,1)S(1)} %copy-done.1, f32[384]{0:T(512)S(1)} %broadcast_multiply_fusion.2, f32[2560]{0:T(1024)S(1)} %copy-done.11, f32[384]{0:T(512)S(1)} %copy-done.13), kind=kLoop, calls=%fused_computation.85 | loop fusion | flops 6881280 | bytes 7877632 | tf_op jit(solution)/shard_map/broadcast_in_dim | solution.py:194
  (157 shorter events, 47.3 us)
Async XLA Ops:
  2.6 3.7 %copy-start.12 = (f32[384]{0:T(512)}, f32[384]{0:T(512)S(1)}, u32[]{:S(2)}) copy-start(f32[384]{0:T(512)S(1)} %add_rsqrt_fusion.1) | copy-start | bytes 4612
  2.7 11.2 %copy-start.9 = (bf16[1,384,2560]{2,1,0:T(8,128)(2,1)S(1)}, bf16[1,384,2560]{2,1,0:T(8,128)(2,1)}, u32[]{:S(2)}) copy-start(bf16[1,384,2560]{2,1,0:T(8,128)(2,1)} %param.10) | copy-start | bytes 5898244
  4.9 10.4 %copy-start.4 = (bf16[384,2560]{1,0:T(8,128)(2,1)}, bf16[384,2560]{1,0:T(8,128)(2,1)S(1)}, u32[]{:S(2)}) copy-start(bf16[384,2560]{1,0:T(8,128)(2,1)S(1)} %fusion.35) | copy-start | bytes 5898244
  4.9 15.7 %copy-start.2 = (bf16[1,384,2560]{2,1,0:T(8,128)(2,1)S(1)}, bf16[1,384,2560]{2,1,0:T(8,128)(2,1)}, u32[]{:S(2)}) copy-start(bf16[1,384,2560]{2,1,0:T(8,128)(2,1)} %param.8) | copy-start | bytes 5898244
  6.3 14.8 %copy-start.16 = (f32[2560]{0:T(1024)S(1)}, f32[2560]{0:T(1024)}, u32[]{:S(2)}) copy-start(f32[2560]{0:T(1024)} %param.12) | copy-start | bytes 30724
  6.3 17.0 %collective-permute-start = (bf16[192,2560]{1,0:T(8,128)(2,1)}, bf16[192,2560]{1,0:T(8,128)(2,1)}, u32[]{:S(2)}, u32[]{:S(2)}) collective-permute-start(bf16[192,2560]{1,0:T(8,128)(2,1)} %get-tuple-element.292), channel_id=1, source_target_pairs={{0,1},{1,2},{2,3},{3,4},{4,5},{5,6},{6,7},{7,8},{8,9},{9,10},{10,1... | collective-permute-start | bytes 2949128 | tf_op jit(solution)/shard_map/ppermute | solution.py:17
  11.0 15.7 %collective-permute-start.1 = (bf16[192,2560]{1,0:T(8,128)(2,1)}, bf16[192,2560]{1,0:T(8,128)(2,1)}, u32[]{:S(2)}, u32[]{:S(2)}) collective-permute-start(bf16[192,2560]{1,0:T(8,128)(2,1)} %get-tuple-element.293), channel_id=1, source_target_pairs={{1,0},{2,1},{3,2},{4,3},{5,4},{6,5},{7,6},{8,7},{9,8},{10,9},{11,1... | collective-permute-start | bytes 2949128 | tf_op jit(solution)/shard_map/ppermute | solution.py:17
  15.3 17.6 %collective-permute-start.2 = (bf16[192,2560]{1,0:T(8,128)(2,1)}, bf16[192,2560]{1,0:T(8,128)(2,1)}, u32[]{:S(2)}, u32[]{:S(2)}) collective-permute-start(bf16[192,2560]{1,0:T(8,128)(2,1)} %get-tuple-element.290), channel_id=1, source_target_pairs={{0,1},{1,2},{2,3},{3,4},{4,5},{5,6},{6,7},{7,8},{8,9},{9,10},{10,1... | collective-permute-start | bytes 2949128 | tf_op jit(solution)/shard_map/ppermute | solution.py:17
  18.0 19.3 %collective-permute-start.3 = (bf16[192,2560]{1,0:T(8,128)(2,1)}, bf16[192,2560]{1,0:T(8,128)(2,1)}, u32[]{:S(2)}, u32[]{:S(2)}) collective-permute-start(bf16[192,2560]{1,0:T(8,128)(2,1)} %get-tuple-element.291), channel_id=1, source_target_pairs={{1,0},{2,1},{3,2},{4,3},{5,4},{6,5},{7,6},{8,7},{9,8},{10,9},{11,1... | collective-permute-start | bytes 2949128 | tf_op jit(solution)/shard_map/ppermute | solution.py:17
  21.0 8.9 %copy-start.14 = (f32[384]{0:T(512)}, f32[384]{0:T(512)S(1)}, u32[]{:S(2)}) copy-start(f32[384]{0:T(512)S(1)} %add_rsqrt_fusion) | copy-start | bytes 4612
  21.1 5.6 %copy-start.5 = (bf16[384,2560]{1,0:T(8,128)(2,1)S(1)}, bf16[384,2560]{1,0:T(8,128)(2,1)}, u32[]{:S(2)}) copy-start(bf16[384,2560]{1,0:T(8,128)(2,1)} %copy-done.4) | copy-start | bytes 5898244
  23.3 13.9 %copy-start.10 = (bf16[1,384,2560]{2,1,0:T(8,128)(2,1)S(1)}, bf16[1,384,2560]{2,1,0:T(8,128)(2,1)}, u32[]{:S(2)}) copy-start(bf16[1,384,2560]{2,1,0:T(8,128)(2,1)} %param.10) | copy-start | bytes 5898244
  49.6 5.9 %copy-start.7 = (bf16[1,576,2560]{2,1,0:T(8,128)(2,1)S(1)}, bf16[1,576,2560]{2,1,0:T(8,128)(2,1)}, u32[]{:S(2)}) copy-start(bf16[1,576,2560]{2,1,0:T(8,128)(2,1)} %get-tuple-element.294) | copy-start | bytes 8847364
  49.6 5.9 %copy-start.8 = (bf16[1,576,2560]{2,1,0:T(8,128)(2,1)S(1)}, bf16[1,576,2560]{2,1,0:T(8,128)(2,1)}, u32[]{:S(2)}) copy-start(bf16[1,576,2560]{2,1,0:T(8,128)(2,1)} %get-tuple-element.295) | copy-start | bytes 8847364
  168.2 10.1 %slice-start.2 = ((s8[7864320]{0:T(1024)(128)(4,1)}), s8[4194304]{0:T(1024)(128)(4,1)S(1)}, s32[]{:S(2)}) async-start(s8[7864320]{0:T(1024)(128)(4,1)} %bitcast.192), calls=%async_computation.2 | async-start | bytes 8388608
  168.2 10.1 %slice-start.3 = ((s8[7864320]{0:T(1024)(128)(4,1)}), s8[3670016]{0:T(1024)(128)(4,1)S(1)}, s32[]{:S(2)}) async-start(s8[7864320]{0:T(1024)(128)(4,1)} %bitcast.192), calls=%async_computation.3 | async-start | bytes 7340032
  172.1 9.8 %slice-start = ((s8[7864320]{0:T(1024)(128)(4,1)}), s8[4194304]{0:T(1024)(128)(4,1)S(1)}, s32[]{:S(2)}) async-start(s8[7864320]{0:T(1024)(128)(4,1)} %bitcast.190), calls=%async_computation | async-start | bytes 8388608
  173.5 18.2 %collective-permute-start.7 = (bf16[192,2560]{1,0:T(8,128)(2,1)}, bf16[192,2560]{1,0:T(8,128)(2,1)S(1)}, u32[]{:S(2)}, u32[]{:S(2)}) collective-permute-start(bf16[192,2560]{1,0:T(8,128)(2,1)} %get-tuple-element.282), channel_id=1, source_target_pairs={{0,1},{1,2},{2,3},{3,4},{4,5},{5,6},{6,7},{7,8},{8,9},{9,10},{10,1... | collective-permute-start | bytes 2949128 | tf_op jit(solution)/shard_map/ppermute | solution.py:17
  175.9 15.6 %collective-permute-start.6 = (bf16[192,2560]{1,0:T(8,128)(2,1)}, bf16[192,2560]{1,0:T(8,128)(2,1)S(1)}, u32[]{:S(2)}, u32[]{:S(2)}) collective-permute-start(bf16[192,2560]{1,0:T(8,128)(2,1)} %get-tuple-element.283), channel_id=1, source_target_pairs={{1,0},{2,1},{3,2},{4,3},{5,4},{6,5},{7,6},{8,7},{9,8},{10,9},{11,1... | collective-permute-start | bytes 2949128 | tf_op jit(solution)/shard_map/ppermute | solution.py:17
  178.4 2.1 copy-start.6
  178.4 3.8 %slice-start.1 = ((s8[7864320]{0:T(1024)(128)(4,1)}), s8[3670016]{0:T(1024)(128)(4,1)S(1)}, s32[]{:S(2)}) async-start(s8[7864320]{0:T(1024)(128)(4,1)} %bitcast.190), calls=%async_computation.1 | async-start | bytes 7340032
  178.9 2.4 copy-start.3
  178.9 2.4 copy-start.15
  182.7 21.1 %collective-permute-start.5 = (bf16[192,2560]{1,0:T(8,128)(2,1)S(1)}, bf16[192,2560]{1,0:T(8,128)(2,1)S(1)}, u32[]{:S(2)}, u32[]{:S(2)}) collective-permute-start(bf16[192,2560]{1,0:T(8,128)(2,1)S(1)} %get-tuple-element.284), channel_id=1, source_target_pairs={{0,1},{1,2},{2,3},{3,4},{4,5},{5,6},{6,7},{7,8},{8,9},{9,10},{10,1... | collective-permute-start | bytes 2949128 | tf_op jit(solution)/shard_map/ppermute | solution.py:17
  185.8 16.2 %collective-permute-start.4 = (bf16[192,2560]{1,0:T(8,128)(2,1)S(1)}, bf16[192,2560]{1,0:T(8,128)(2,1)S(1)}, u32[]{:S(2)}, u32[]{:S(2)}) collective-permute-start(bf16[192,2560]{1,0:T(8,128)(2,1)S(1)} %get-tuple-element.285), channel_id=1, source_target_pairs={{1,0},{2,1},{3,2},{4,3},{5,4},{6,5},{7,6},{8,7},{9,8},{10,9},{11,1... | collective-permute-start | bytes 2949128 | tf_op jit(solution)/shard_map/ppermute | solution.py:17
  203.8 2.3 copy-start.1
  203.8 2.3 copy-start.11
  203.8 2.3 copy-start.13
  204.2 1.9 copy-start
where the time goes:
time: 299 us; the launch traced here: 298 us
  blocking collectives  84.7 us (28%)
  local copies, waits for them, and re-layouts  60 us (20%)
  matrix products  53 us (18%)
  other arithmetic  51.3 us (17%)
  waiting for transfers between devices  24.2 us (8%)
  starting transfers between devices  22.6 us (8%)
    psum x1, blocking collectives, per_device(): q_sum, k_sum = lax.psum((q_part, k_part), ('dp', 'space'))  84.7 us
    ppermute x8, waiting for transfers between devices, from_behind(): return lax.ppermute(block, axis, route)  24.2 us
    ppermute x8, starting transfers between devices, from_behind(): return lax.ppermute(block, axis, route)  22.6 us
    dot_general x5, matrix products, attend(): jnp.einsum('tqhd,tkhd->thqk', grad4, values4, preferred_element_type=jnp....  10.8 us
    dot_general x5, matrix products, attend(): jnp.einsum('thqk,tkhd->tqhd', probs_b, values4, preferred_element_type=jn...  10.7 us
    sub x5, other arithmetic, attend(): expo = jnp.exp(scores - row_top)  10.1 us
    another operation x12, local copies, waits for them, and re-layouts  10 us
    dot_general x5, matrix products, attend(): jnp.einsum('tqhd,tkhd->thqk', query4, keys4, preferred_element_type=jnp.f...  9.95 us
  transfers between devices with their start and end apart: 8, of which 5 were waited for; matrix products, arithmetic and copies ran while one was open for 4% of the time, Pallas kernels for 0%

commit v1 on v0

v1 whole, which is shorter than its diff:
```python
import functools
import math

import jax
import jax.numpy as jnp
from jax import lax
from jax.experimental import pallas as pl
from jax.experimental.pallas import tpu as pltpu
from jax.sharding import PartitionSpec as P

HS = 128
EPS = 1e-06
SCALE = HS ** (-0.5)
LOG_SCALE = SCALE * math.log2(math.e)
LAG = 4
CHUNK = 32
MESH = pl.DeviceIdType.MESH
NT = (((1,), (1,)), ((), ()))
NN = (((1,), (0,)), ((), ()))


def dot(a, b, dims):
    return lax.dot_general(a, b, dims, preferred_element_type=jnp.float32)


def sum_stages(dp, space):
    def pairs(axis, bits):
        return [(axis, tuple(bits[i : i + 2])) for i in range(0, len(bits), 2)]

    space_bits = list(range(space.bit_length() - 1))
    if len(space_bits) == 4:
        space_bits = [0, 3, 1, 2]
    return pairs("space", space_bits) + pairs("dp", list(range(dp.bit_length() - 1)))


def group_place(index, bits):
    digits = [(index // 2**bit) % 2 for bit in bits]
    place = sum(digit * 2**at for at, digit in enumerate(digits))
    base = index - sum(digit * 2**bit for digit, bit in zip(digits, bits))

    def member(other):
        return base + sum(((other // 2**at) % 2) * 2**bit for at, bit in enumerate(bits))

    return place, member


def kernel(
    stages,
    space,
    factor,
    q_hbm,
    k_hbm,
    v_hbm,
    g_hbm,
    q_gain,
    k_gain,
    k_out,
    v_out,
    q_gain_out,
    k_gain_out,
    q_raw,
    k_raw,
    value,
    own,
    key,
    k_inv,
    near,
    extra,
    e_own,
    p_own,
    e_near,
    p_near,
    e_extra,
    p_extra,
    dk,
    dv,
    v_grad,
    row_dot,
    own_stat,
    near_stat,
    extra_stat,
    to_left,
    to_right,
    from_left,
    from_right,
    gain_part,
    gain_box,
    load_sem,
    g_sem,
    near_send,
    near_recv,
    extra_send,
    extra_recv,
    stat_send,
    stat_recv,
    v_sem,
    k_sem,
    gain_send,
    gain_recv,
):
    me = lax.axis_index("space")
    heads, _, rows, _ = own.shape
    tile = rows // 2
    features = heads * HS
    low, high = pl.ds(0, tile), pl.ds(tile, tile)
    first, second = pl.ds(0, HS), pl.ds(HS, HS)
    has_left, has_right = me > 0, me < space - 1
    extra_left, extra_right = me == 1, me == space - 2
    is_extra = jnp.logical_or(extra_left, extra_right)
    left, right = {"space": me - 1}, {"space": me + 1}

    def columns(head):
        return pl.ds(pl.multiple_of(head * HS, HS), HS)

    load_q = pltpu.make_async_copy(q_hbm, q_raw, load_sem.at[0])
    load_k = pltpu.make_async_copy(k_hbm, k_raw, load_sem.at[1])
    load_v = pltpu.make_async_copy(v_hbm, value, load_sem.at[2])

    def load_g(head):
        return pltpu.make_async_copy(g_hbm.at[:, columns(head)], own.at[head, 1], g_sem.at[head])

    load_q.start()

    @pl.loop(0, heads)
    def _(head):
        load_g(head).start()

    load_k.start()
    load_v.start()

    barrier = pltpu.get_barrier_semaphore()

    @pl.when(has_left)
    def _():
        pl.semaphore_signal(barrier, inc=1, device_id=left, device_id_type=MESH)

    @pl.when(has_right)
    def _():
        pl.semaphore_signal(barrier, inc=1, device_id=right, device_id_type=MESH)

    partners = 0
    for axis, bits in stages:
        place, member = group_place(lax.axis_index(axis), bits)
        size = 2 ** len(bits)
        for step in range(1, size):
            pl.semaphore_signal(
                barrier,
                inc=1,
                device_id={axis: member((place + step) % size)},
                device_id_type=MESH,
            )
            partners += 1

    zeros = jnp.zeros((2, tile, HS), jnp.bfloat16)

    @pl.loop(0, heads)
    def _(head):
        near[head, :, low, first] = zeros
        near[head, :, high, second] = zeros

        @pl.when(jnp.logical_not(has_left))
        def _():
            near[head, :, high, first] = zeros
            from_left[head] = jnp.zeros(from_left.shape[1:], jnp.float32)

        @pl.when(jnp.logical_not(has_right))
        def _():
            near[head, :, low, second] = zeros
            from_right[head] = jnp.zeros(from_right.shape[1:], jnp.float32)

        @pl.when(is_extra)
        def _():
            extra[head, :, low, second] = zeros
            extra[head, :, high, first] = zeros

        @pl.when(jnp.logical_and(is_extra, jnp.logical_not(extra_left)))
        def _():
            extra[head, :, low, first] = zeros

        @pl.when(jnp.logical_and(is_extra, jnp.logical_not(extra_right)))
        def _():
            extra[head, :, high, second] = zeros

    extra_stat[...] = jnp.zeros_like(extra_stat)
    row_dot[...] = jnp.zeros_like(row_dot)
    gain_part[...] = jnp.zeros_like(gain_part)

    load_q.wait()

    def normalize(raw, gain, row_begin, put):
        span = pl.ds(pl.multiple_of(row_begin, CHUNK), CHUNK)
        total = jnp.zeros((CHUNK, HS), jnp.float32)
        for head in range(heads):
            wide = raw[span, head * HS : (head + 1) * HS].astype(jnp.float32)
            total = total + wide * wide
        mean = jnp.sum(total, axis=-1, keepdims=True) * (1.0 / features)
        inverse = lax.rsqrt(mean + EPS)
        for head in range(heads):
            wide = raw[span, head * HS : (head + 1) * HS].astype(jnp.float32)
            put(
                head,
                span,
                (wide * inverse * gain[:, head * HS : (head + 1) * HS]).astype(jnp.bfloat16),
            )
        return span, inverse

    def put_query(head, span, block):
        own[head, 0, span, :] = block

    def put_key(head, span, block):
        key[head, span, :] = block

    @pl.loop(0, rows // CHUNK)
    def _(chunk):
        normalize(q_raw, q_gain, chunk * CHUNK, put_query)

    count = partners + has_left.astype(jnp.int32) + has_right.astype(jnp.int32)
    pl.semaphore_wait(barrier, count)

    def near_to_right(head):
        return pltpu.make_async_remote_copy(
            src_ref=own.at[head, :, high, :],
            dst_ref=near.at[head, :, high, first],
            send_sem=near_send.at[0, head],
            recv_sem=near_recv.at[0, head],
            device_id=right,
            device_id_type=MESH,
        )

    def near_to_left(head):
        return pltpu.make_async_remote_copy(
            src_ref=own.at[head, :, low, :],
            dst_ref=near.at[head, :, low, second],
            send_sem=near_send.at[1, head],
            recv_sem=near_recv.at[1, head],
            device_id=left,
            device_id_type=MESH,
        )

    def extra_to_right(head):
        return pltpu.make_async_remote_copy(
            src_ref=own.at[head, :, low, :],
            dst_ref=extra.at[head, :, low, first],
            send_sem=extra_send.at[0, head],
            recv_sem=extra_recv.at[0, head],
            device_id=right,
            device_id_type=MESH,
        )

    def extra_to_left(head):
        return pltpu.make_async_remote_copy(
            src_ref=own.at[head, :, high, :],
            dst_ref=extra.at[head, :, high, second],
            send_sem=extra_send.at[1, head],
            recv_sem=extra_recv.at[1, head],
            device_id=left,
            device_id_type=MESH,
        )

    @pl.loop(0, heads)
    def _(head):
        load_g(head).wait()

        @pl.when(has_right)
        def _():
            near_to_right(head).start()

        @pl.when(has_left)
        def _():
            near_to_left(head).start()

        @pl.when(jnp.logical_not(has_left))
        def _():
            extra_to_right(head).start()

        @pl.when(jnp.logical_not(has_right))
        def _():
            extra_to_left(head).start()

    load_k.wait()

    @pl.loop(0, rows // CHUNK)
    def _(chunk):
        span, inverse = normalize(k_raw, k_gain, chunk * CHUNK, put_key)
        k_inv[span, :] = jnp.broadcast_to(inverse, (CHUNK, HS))

    load_v.wait()

    in_low = lax.broadcasted_iota(jnp.int32, (1, rows), 1) < tile

    def stat_to_left(head):
        return pltpu.make_async_remote_copy(
            src_ref=to_left.at[head],
            dst_ref=from_right.at[head],
            send_sem=stat_send.at[0, head],
            recv_sem=stat_recv.at[0, head],
            device_id=left,
            device_id_type=MESH,
        )

    def stat_to_right(head):
        return pltpu.make_async_remote_copy(
            src_ref=to_right.at[head],
            dst_ref=from_left.at[head],
            send_sem=stat_send.at[1, head],
            recv_sem=stat_recv.at[1, head],
            device_id=right,
            device_id_type=MESH,
        )

    def wide_pair(block):
        return jnp.concatenate([block[:tile], block[tile:]], axis=1)

    def scores(keys, values, queries, grads, e_ref, p_ref):
        score = dot(keys, queries, NT)
        top = jnp.max(score, axis=0, keepdims=True)
        expo = jnp.exp2((score - top) * LOG_SCALE)
        dprobs = dot(values, grads, NT)
        e_ref[...] = expo
        p_ref[...] = dprobs
        return (
            top,
            jnp.sum(expo, axis=0, keepdims=True),
            jnp.sum(expo * dprobs, axis=0, keepdims=True),
        )

    def put_stat(ref, slot, stat):
        for at, row in enumerate(stat):
            ref[slot, at : at + 1, :] = row

    def forward(head):
        slot = head % (LAG + 1)
        keys, values = key[head], value[:, columns(head)]
        stat = scores(keys, values, own[head, 0], own[head, 1], e_own.at[slot], p_own.at[slot])
        put_stat(own_stat, head, stat)
        stat = scores(
            wide_pair(keys),
            wide_pair(values),
            near[head, 0],
            near[head, 1],
            e_near.at[slot],
            p_near.at[slot],
        )
        put_stat(near_stat, head, stat)

    def forward_extra(head):
        slot = head % (LAG + 1)
        stat = scores(
            wide_pair(key[head]),
            wide_pair(value[:, columns(head)]),
            extra[head, 0],
            extra[head, 1],
            e_extra.at[slot],
            p_extra.at[slot],
        )
        put_stat(extra_stat, head, stat)

    def tell(head):
        near_now, extra_now = near_stat[head], extra_stat[head]
        to_left[head, 0:8, :] = own_stat[head]
        to_left[head, 8:16, :] = jnp.where(in_low, extra_now, near_now)
        to_right[head, 0:8, :] = own_stat[head]
        to_right[head, 8:16, :] = jnp.where(in_low, near_now, extra_now)

        @pl.when(has_left)
        def _():
            stat_to_left(head).start()

        @pl.when(has_right)
        def _():
            stat_to_right(head).start()

    def merge(mine, other):
        top = jnp.maximum(mine[0:1], other[0:1])
        a = jnp.exp2((mine[0:1] - top) * LOG_SCALE)
        b = jnp.exp2((other[0:1] - top) * LOG_SCALE)
        inverse = 1.0 / (mine[1:2] * a + other[1:2] * b)
        return a * inverse, (mine[2:3] * a + other[2:3] * b) * inverse

    def backward_terms(e_ref, p_ref, mine, other, queries, grads):
        weight, delta = merge(mine, other)
        probs = e_ref[...] * weight
        dscores = (probs * (p_ref[...] - delta)).astype(jnp.bfloat16)
        return dot(dscores, queries, NN), dot(probs.astype(jnp.bfloat16), grads, NN)

    def backward(head):
        slot = head % (LAG + 1)
        left_stat, right_stat = from_left[head], from_right[head]
        from_low = jnp.logical_and(jnp.logical_or(in_low, me == space - 1), me > 0)
        other = jnp.where(from_low, left_stat[8:16], right_stat[8:16])
        dkey, dvalue = backward_terms(
            e_own.at[slot], p_own.at[slot], own_stat[head], other, own[head, 0], own[head, 1]
        )
        other = jnp.where(in_low, right_stat[0:8], left_stat[0:8])
        near_dkey, near_dvalue = backward_terms(
            e_near.at[slot], p_near.at[slot], near_stat[head], other, near[head, 0], near[head, 1]
        )
        dk[head, low, :] = dkey[:tile] + near_dkey[:, :HS]
        dk[head, high, :] = dkey[tile:] + near_dkey[:, HS:]
        dv[low, :] = dvalue[:tile] + near_dvalue[:, :HS]
        dv[high, :] = dvalue[tile:] + near_dvalue[:, HS:]

    def backward_extra(head):
        slot = head % (LAG + 1)
        other = jnp.where(in_low, from_left[head, 0:8, :], from_right[head, 0:8, :])
        dkey, dvalue = backward_terms(
            e_extra.at[slot],
            p_extra.at[slot],
            extra_stat[head],
            other,
            extra[head, 0],
            extra[head, 1],
        )
        dk[head, low, :] += dkey[:, :HS]
        dk[head, high, :] += dkey[:, HS:]
        dv[low, :] += dvalue[:, :HS]
        dv[high, :] += dvalue[:, HS:]

    def store_v(head):
        return pltpu.make_async_copy(v_grad.at[head], v_out.at[:, columns(head)], v_sem.at[head])

    def finish(head):
        v_grad[head] = dv[...].astype(jnp.bfloat16)
        store_v(head).start()
        total = dk[head] * SCALE
        kn = k_raw[:, columns(head)].astype(jnp.float32) * k_inv[...]
        gain_part[pl.ds(head, 1), :] = jnp.sum(total * kn, axis=0, keepdims=True)
        dkn = total * k_gain[:, columns(head)]
        dk[head] = dkn
        row_dot[...] += dkn * kn

    def wait_near(head):
        @pl.when(has_left)
        def _():
            near_to_right(head).wait_recv()

        @pl.when(has_right)
        def _():
            near_to_left(head).wait_recv()

        @pl.when(extra_left)
        def _():
            extra_to_right(head).wait_recv()

        @pl.when(extra_right)
        def _():
            extra_to_left(head).wait_recv()

    def wait_stat(head):
        @pl.when(has_left)
        def _():
            stat_to_right(head).wait_recv()

        @pl.when(has_right)
        def _():
            stat_to_left(head).wait_recv()

    @pl.loop(0, LAG)
    def _(head):
        wait_near(head)
        forward(head)

        @pl.when(is_extra)
        def _():
            forward_extra(head)

        tell(head)

    @pl.loop(LAG, heads)
    def _(head):
        behind = head - LAG
        wait_near(head)
        wait_stat(behind)
        forward(head)
        backward(behind)

        @pl.when(is_extra)
        def _():
            forward_extra(head)
            backward_extra(behind)

        tell(head)
        finish(behind)

    @pl.loop(heads - LAG, heads)
    def _(head):
        wait_stat(head)
        backward(head)

        @pl.when(is_extra)
        def _():
            backward_extra(head)

        finish(head)

    mean = jnp.sum(row_dot[...], axis=-1, keepdims=True) * (1.0 / features)
    row_dot[...] = jnp.broadcast_to(mean, row_dot.shape)

    def store_k(head):
        columns_now = slice(head * HS, (head + 1) * HS)
        return pltpu.make_async_copy(
            q_raw.at[:, columns_now], k_out.at[:, columns_now], k_sem.at[head]
        )

    def key_pass(head):
        kn = k_raw[:, head * HS : (head + 1) * HS].astype(jnp.float32) * k_inv[...]
        q_raw[:, head * HS : (head + 1) * HS] = (
            k_inv[...] * (dk[head] - kn * row_dot[...])
        ).astype(jnp.bfloat16)
        store_k(head).start()

    total = gain_part[...]
    done = 0
    for at, (axis, bits) in enumerate(stages):
        place, member = group_place(lax.axis_index(axis), bits)
        size = 2 ** len(bits)
        gain_box[at, pl.ds(place, 1)] = total[None]
        copies = [
            pltpu.make_async_remote_copy(
                src_ref=gain_box.at[at, place],
                dst_ref=gain_box.at[at, place],
                send_sem=gain_send.at[at, step],
                recv_sem=gain_recv.at[at, step],
                device_id={axis: member((place + step) % size)},
                device_id_type=MESH,
            )
            for step in range(1, size)
        ]
        for copy in copies:
            copy.start()
        until = heads * (at + 1) // len(stages)
        for head in range(done, until):
            key_pass(head)
        done = until
        for step in range(1, size):
            source = (place + size - step) % size
            pltpu.make_async_remote_copy(
                src_ref=gain_box.at[at, place],
                dst_ref=gain_box.at[at, source],
                send_sem=gain_send.at[at, step],
                recv_sem=gain_recv.at[at, step],
                device_id={axis: member((place + step) % size)},
                device_id_type=MESH,
            ).wait_recv()
        total = gain_box[at, 0]
        for other in range(1, size):
            total = total + gain_box[at, other]
        for copy in copies:
            copy.wait_send()

    result = total[:heads] * factor
    k_gain_out[...] = result
    q_gain_out[...] = result
    for head in range(heads):
        cut = slice(head * HS, (head + 1) * HS)
        q_gain_out[head : head + 1, :] = (
            result[head : head + 1] * k_gain[:, cut] / q_gain[:, cut]
        )

    @pl.loop(0, heads)
    def _(head):
        store_v(head).wait()

        @pl.when(has_right)
        def _():
            near_to_right(head).wait_send()
            stat_to_right(head).wait_send()

        @pl.when(has_left)
        def _():
            near_to_left(head).wait_send()
            stat_to_left(head).wait_send()

        @pl.when(jnp.logical_not(has_left))
        def _():
            extra_to_right(head).wait_send()

        @pl.when(jnp.logical_not(has_right))
        def _():
            extra_to_left(head).wait_send()

    for head in range(heads):
        store_k(head).wait()


def per_device(queries_raw, keys_raw, values, out_grad, q_gain, k_gain):
    _, rows, features = queries_raw.shape
    heads = features // HS
    tile = rows // 2
    dp, space = lax.axis_size("dp"), lax.axis_size("space")
    stages = sum_stages(dp, space)
    factor = (dp * space * rows) ** (-0.5)
    slots = LAG + 1
    bf16, f32 = jnp.bfloat16, jnp.float32
    padded = (heads + 7) // 8 * 8
    hbm = pl.BlockSpec(memory_space=pl.ANY)
    vmem = pl.BlockSpec(memory_space=pltpu.VMEM)
    dma = pltpu.SemaphoreType.DMA
    key_grad, value_grad, q_sum, k_sum = pl.pallas_call(
        functools.partial(kernel, stages, space, factor),
        out_shape=(
            jax.ShapeDtypeStruct((rows, features), bf16),
            jax.ShapeDtypeStruct((rows, features), bf16),
            jax.ShapeDtypeStruct((heads, HS), f32),
            jax.ShapeDtypeStruct((heads, HS), f32),
        ),
        in_specs=[hbm] * 4 + [vmem] * 2,
        out_specs=(hbm, hbm, vmem, vmem),
        scratch_shapes=[
            pltpu.VMEM((rows, features), bf16),
            pltpu.VMEM((rows, features), bf16),
            pltpu.VMEM((rows, features), bf16),
            pltpu.VMEM((heads, 2, rows, HS), bf16),
            pltpu.VMEM((heads, rows, HS), bf16),
            pltpu.VMEM((rows, HS), f32),
            pltpu.VMEM((heads, 2, rows, 2 * HS), bf16),
            pltpu.VMEM((heads, 2, rows, 2 * HS), bf16),
            pltpu.VMEM((slots, rows, rows), f32),
            pltpu.VMEM((slots, rows, rows), f32),
            pltpu.VMEM((slots, tile, rows), f32),
            pltpu.VMEM((slots, tile, rows), f32),
            pltpu.VMEM((slots, tile, rows), f32),
            pltpu.VMEM((slots, tile, rows), f32),
            pltpu.VMEM((heads, rows, HS), f32),
            pltpu.VMEM((rows, HS), f32),
            pltpu.VMEM((heads, rows, HS), bf16),
            pltpu.VMEM((rows, HS), f32),
            pltpu.VMEM((heads, 8, rows), f32),
            pltpu.VMEM((heads, 8, rows), f32),
            pltpu.VMEM((heads, 8, rows), f32),
            pltpu.VMEM((heads, 16, rows), f32),
            pltpu.VMEM((heads, 16, rows), f32),
            pltpu.VMEM((heads, 16, rows), f32),
            pltpu.VMEM((heads, 16, rows), f32),
            pltpu.VMEM((padded, HS), f32),
            pltpu.VMEM((len(stages), 4, padded, HS), f32),
            dma((3,)),
            dma((heads,)),
            dma((2, heads)),
            dma((2, heads)),
            dma((2, heads)),
            dma((2, heads)),
            dma((2, heads)),
            dma((2, heads)),
            dma((heads,)),
            dma((heads,)),
            dma((len(stages), 4)),
            dma((len(stages), 4)),
        ],
        compiler_params=pltpu.CompilerParams(
            collective_id=0, has_side_effects=True, vmem_limit_bytes=60 * 2**20
        ),
    )(
        queries_raw[0],
        keys_raw[0],
        values[0],
        out_grad[0],
        q_gain.reshape(1, features),
        k_gain.reshape(1, features),
    )
    return key_grad[None], value_grad[None], q_sum.reshape(features), k_sum.reshape(features)


def solution(mesh):
    split = P("dp", "space", None)
    return jax.shard_map(
        per_device,
        mesh=mesh,
        in_specs=(split, split, split, split, P(), P()),
        out_specs=(split, split, P(), P()),
        check_vma=False,
    )
```

time: 299 us -> 89 us (0.30)
  blocking collectives: 84.7 us -> 0 us
  Pallas kernels: 0 us -> 79.4 us
  matrix products: 53 us -> 0 us
  local copies, waits for them, and re-layouts: 60 us -> 8.2 us
  other arithmetic: 51.3 us -> 0 us
  waiting for transfers between devices: 24.2 us -> 0 us
  starting transfers between devices: 22.6 us -> 0 us
    psum x1 -> x0, blocking collectives: 84.7 us -> none  [per_device(): q_sum, k_sum = lax.psum((q_part, k_part), ('dp', 'space'))]
    pallas_call x0 -> x1, Pallas kernels: none -> 79.4 us  [per_device(): pl.pallas_call(functools.partial(kernel, stages, space, factor), out_shap...]
    dot_general x40 -> x0, matrix products: 53 us -> none  [the longest x5 10.8 us: attend(): jnp.einsum('tqhd,tkhd->thqk', grad4, values4, preferred_element_type=jnp....]
    ppermute x8 -> x0, waiting for transfers between devices: 24.2 us -> none  [from_behind(): return lax.ppermute(block, axis, route)]
    ppermute x8 -> x0, starting transfers between devices: 22.6 us -> none  [from_behind(): return lax.ppermute(block, axis, route)]
    dynamic_update_slice x25 -> x0, local copies, waits for them, and re-layouts: 19.9 us -> none  [the longest x5 6.72 us: reader_step(): dkey_all = lax.dynamic_update_slice_in_dim(dkey_all, group_key, column, 1)]
    another operation x13 -> x0, local copies, waits for them, and re-layouts: 19.1 us -> none
    another operation x4 -> x0, other arithmetic: 13.3 us -> none  [the longest x1 5.91 us: per_device(): jnp.stack([lax.dynamic_slice_in_dim(near_values, offsets[which_tile] * R,...]
  transfers between devices with their start and end apart: 8 -> 0, of which waited for: 5 -> 0; matrix products, arithmetic and copies ran while one was open for 4% -> 0% of each run, Pallas kernels for 0% -> 0%
where the time goes in v1:
time: 89 us; the launch traced here: 88.2 us
  Pallas kernels  79.4 us (89%)
  local copies, waits for them, and re-layouts  8.2 us (9%)
    pallas_call x1, Pallas kernels, per_device(): pl.pallas_call(functools.partial(kernel, stages, space, factor), out_shap...  79.4 us
    unnamed x10, local copies, waits for them, and re-layouts  5.57 us

profile of v1, /device:TPU:1, one launch (start us, length us, event | category | flops | bytes accessed | tf_op | source)
XLA Modules:
  0.0 88.2 jit_solution(10694581640270187385)
XLA Ops:
  0.6 1.3 %reshape.20.q_gain = f32[1,2560]{1,0:T(1,128)} reshape(f32[2560]{0:T(1024)} %param.10) | data formatting | bytes 20480 | tf_op jit(solution)/shard_map/reshape | solution.py:658
  1.9 1.3 %reshape.21.k_gain = f32[1,2560]{1,0:T(1,128)} reshape(f32[2560]{0:T(1024)} %param.11) | data formatting | bytes 20480 | tf_op jit(solution)/shard_map/reshape | solution.py:659
  3.3 79.4 %shard_map.93 = (bf16[384,2560]{1,0:T(8,128)(2,1)}, bf16[384,2560]{1,0:T(8,128)(2,1)}, f32[20,128]{1,0:T(8,128)}, f32[20,128]{1,0:T(8,128)}) custom-call(bf16[384,2560]{1,0:T(8,128)(2,1)} %bitcast.8, bf16[384,2560]{1,0:T(8,128)(2,1)} %bitcast.9, bf16[384,2560]{1,0:T(8,128)(2,1)} %bitcast.10, bf16[384,2560]{1,0:T(8,128)(2,1)} %bitcast.11, ...), custom_call_target="tpu_custom_call" | custom-call | tf_op jit(solution)/shard_map/pallas_call | solution.py:599
  82.6 0.0 copy-start
  82.6 3.1 %copy.14 = bf16[1,384,2560]{2,1,0:T(8,128)(2,1)} copy(bf16[1,384,2560]{2,1,0:T(8,128)(2,1)} %bitcast.13) | data formatting | bytes 3932160
  85.7 0.0 copy-done
  85.7 0.0 copy-start.2
  85.7 0.0 copy-start.1
  85.7 1.3 %copy.15 = bf16[1,384,2560]{2,1,0:T(8,128)(2,1)} copy(bf16[1,384,2560]{2,1,0:T(8,128)(2,1)S(1)} %bitcast.12) | data formatting | bytes 3932160
  87.0 0.0 copy-done.2
  87.0 0.6 copy.16
  87.6 0.0 copy-done.1
  87.6 0.6 copy.17
Async XLA Ops:
  82.6 3.1 %copy-start = (bf16[384,2560]{1,0:T(8,128)(2,1)S(1)}, bf16[384,2560]{1,0:T(8,128)(2,1)}, u32[]{:S(2)}) copy-start(bf16[384,2560]{1,0:T(8,128)(2,1)} %get-tuple-element.9) | copy-start | bytes 5898244
  85.7 1.3 %copy-start.2 = (f32[20,128]{1,0:T(8,128)S(1)}, f32[20,128]{1,0:T(8,128)}, u32[]{:S(2)}) copy-start(f32[20,128]{1,0:T(8,128)} %get-tuple-element.10) | copy-start | bytes 30724
  85.7 1.9 %copy-start.1 = (f32[20,128]{1,0:T(8,128)S(1)}, f32[20,128]{1,0:T(8,128)}, u32[]{:S(2)}) copy-start(f32[20,128]{1,0:T(8,128)} %get-tuple-element.11) | copy-start | bytes 30724

commit v2 on v1

--- a/solution.py
+++ b/solution.py
@@ -13,6 +13,8 @@
 SCALE = HS ** (-0.5)
 LOG_SCALE = SCALE * math.log2(math.e)
 LAG = 4
+FINISH_LAG = 2
+LEAD = 5
 CHUNK = 32
 MESH = pl.DeviceIdType.MESH
 NT = (((1,), (1,)), ((), ()))
@@ -52,8 +54,8 @@
     k_hbm,
     v_hbm,
     g_hbm,
-    q_gain,
-    k_gain,
+    q_gain_flat,
+    k_gain_flat,
     k_out,
     v_out,
     q_gain_out,
@@ -65,32 +67,35 @@
     key,
     k_inv,
     near,
-    extra,
+    edge_keys,
     e_own,
     p_own,
     e_near,
     p_near,
-    e_extra,
-    p_extra,
     dk,
     dv,
     v_grad,
     row_dot,
     own_stat,
     near_stat,
-    extra_stat,
     to_left,
     to_right,
     from_left,
     from_right,
+    edge_out,
+    edge_in,
     gain_part,
     gain_box,
+    q_gain,
+    k_gain,
     load_sem,
     g_sem,
     near_send,
     near_recv,
-    extra_send,
-    extra_recv,
+    keys_send,
+    keys_recv,
+    edge_send,
+    edge_recv,
     stat_send,
     stat_recv,
     v_sem,
@@ -105,8 +110,7 @@
     low, high = pl.ds(0, tile), pl.ds(tile, tile)
     first, second = pl.ds(0, HS), pl.ds(HS, HS)
     has_left, has_right = me > 0, me < space - 1
-    extra_left, extra_right = me == 1, me == space - 2
-    is_extra = jnp.logical_or(extra_left, extra_right)
+    beside_first, beside_last = me == 1, me == space - 2
     left, right = {"space": me - 1}, {"space": me + 1}
 
     def columns(head):
@@ -158,32 +162,13 @@
         near[head, :, low, first] = zeros
         near[head, :, high, second] = zeros
 
-        @pl.when(jnp.logical_not(has_left))
-        def _():
-            near[head, :, high, first] = zeros
-            from_left[head] = jnp.zeros(from_left.shape[1:], jnp.float32)
-
-        @pl.when(jnp.logical_not(has_right))
-        def _():
-            near[head, :, low, second] = zeros
-            from_right[head] = jnp.zeros(from_right.shape[1:], jnp.float32)
-
-        @pl.when(is_extra)
-        def _():
-            extra[head, :, low, second] = zeros
-            extra[head, :, high, first] = zeros
-
-        @pl.when(jnp.logical_and(is_extra, jnp.logical_not(extra_left)))
-        def _():
-            extra[head, :, low, first] = zeros
-
-        @pl.when(jnp.logical_and(is_extra, jnp.logical_not(extra_right)))
-        def _():
-            extra[head, :, high, second] = zeros
-
-    extra_stat[...] = jnp.zeros_like(extra_stat)
     row_dot[...] = jnp.zeros_like(row_dot)
     gain_part[...] = jnp.zeros_like(gain_part)
+
+    for head in range(heads):
+        cut = slice(head * HS, (head + 1) * HS)
+        q_gain[:, cut] = q_gain_flat[cut].reshape(1, HS)
+        k_gain[:, cut] = k_gain_flat[cut].reshape(1, HS)
 
     load_q.wait()
 
@@ -237,45 +222,68 @@
             device_id_type=MESH,
         )
 
-    def extra_to_right(head):
+    def keys_to_first(head):
+        return [
+            pltpu.make_async_remote_copy(
+                src_ref=source,
+                dst_ref=edge_keys.at[head, at],
+                send_sem=keys_send.at[at, head],
+                recv_sem=keys_recv.at[at, head],
+                device_id=left,
+                device_id_type=MESH,
+            )
+            for at, source in enumerate((key.at[head, low, :], value.at[low, columns(head)]))
+        ]
+
+    def keys_to_last(head):
+        return [
+            pltpu.make_async_remote_copy(
+                src_ref=source,
+                dst_ref=edge_keys.at[head, at],
+                send_sem=keys_send.at[at, head],
+                recv_sem=keys_recv.at[at, head],
+                device_id=right,
+                device_id_type=MESH,
+            )
+            for at, source in enumerate((key.at[head, high, :], value.at[high, columns(head)]))
+        ]
+
+    def edge_copy(head, device):
         return pltpu.make_async_remote_copy(
-            src_ref=own.at[head, :, low, :],
-            dst_ref=extra.at[head, :, low, first],
-            send_sem=extra_send.at[0, head],
-            recv_sem=extra_recv.at[0, head],
-            device_id=right,
+            src_ref=edge_out.at[head],
+            dst_ref=edge_in.at[head],
+            send_sem=edge_send.at[head],
+            recv_sem=edge_recv.at[head],
+            device_id=device,
             device_id_type=MESH,
         )
 
-    def extra_to_left(head):
-        return pltpu.make_async_remote_copy(
-            src_ref=own.at[head, :, high, :],
-            dst_ref=extra.at[head, :, high, second],
-            send_sem=extra_send.at[1, head],
-            recv_sem=extra_recv.at[1, head],
-            device_id=left,
-            device_id_type=MESH,
-        )
+    def send_near(head):
+        @pl.when(has_right)
+        def _():
+            near_to_right(head).start()
+
+        @pl.when(has_left)
+        def _():
+            near_to_left(head).start()
 
     @pl.loop(0, heads)
     def _(head):
         load_g(head).wait()
 
-        @pl.when(has_right)
-        def _():
-            near_to_right(head).start()
-
-        @pl.when(has_left)
-        def _():
-            near_to_left(head).start()
-
+    @pl.loop(0, LEAD)
+    def _(head):
+        send_near(head)
+
+    @pl.loop(0, heads)
+    def _(head):
         @pl.when(jnp.logical_not(has_left))
         def _():
-            extra_to_right(head).start()
+            near[head, :, high, first] = own[head, :, low, :]
 
         @pl.when(jnp.logical_not(has_right))
         def _():
-            extra_to_left(head).start()
+            near[head, :, low, second] = own[head, :, high, :]
 
     load_k.wait()
 
@@ -285,6 +293,20 @@
         k_inv[span, :] = jnp.broadcast_to(inverse, (CHUNK, HS))
 
     load_v.wait()
+
+    @pl.when(beside_first)
+    def _():
+        @pl.loop(0, heads)
+        def _(head):
+            for copy in keys_to_first(head):
+                copy.start()
+
+    @pl.when(beside_last)
+    def _():
+        @pl.loop(0, heads)
+        def _(head):
+            for copy in keys_to_last(head):
+                copy.start()
 
     in_low = lax.broadcasted_iota(jnp.int32, (1, rows), 1) < tile
 
@@ -308,8 +330,14 @@
             device_id_type=MESH,
         )
 
-    def wide_pair(block):
-        return jnp.concatenate([block[:tile], block[tile:]], axis=1)
+    def wide_pair(block, edge):
+        return jnp.concatenate(
+            [
+                jnp.where(has_left, block[:tile], edge),
+                jnp.where(has_right, block[tile:], edge),
+            ],
+            axis=1,
+        )
 
     def scores(keys, values, queries, grads, e_ref, p_ref):
         score = dot(keys, queries, NT)
@@ -334,8 +362,8 @@
         stat = scores(keys, values, own[head, 0], own[head, 1], e_own.at[slot], p_own.at[slot])
         put_stat(own_stat, head, stat)
         stat = scores(
-            wide_pair(keys),
-            wide_pair(values),
+            wide_pair(keys, edge_keys[head, 0]),
+            wide_pair(values, edge_keys[head, 1]),
             near[head, 0],
             near[head, 1],
             e_near.at[slot],
@@ -343,24 +371,12 @@
         )
         put_stat(near_stat, head, stat)
 
-    def forward_extra(head):
-        slot = head % (LAG + 1)
-        stat = scores(
-            wide_pair(key[head]),
-            wide_pair(value[:, columns(head)]),
-            extra[head, 0],
-            extra[head, 1],
-            e_extra.at[slot],
-            p_extra.at[slot],
-        )
-        put_stat(extra_stat, head, stat)
-
     def tell(head):
-        near_now, extra_now = near_stat[head], extra_stat[head]
-        to_left[head, 0:8, :] = own_stat[head]
-        to_left[head, 8:16, :] = jnp.where(in_low, extra_now, near_now)
-        to_right[head, 0:8, :] = own_stat[head]
-        to_right[head, 8:16, :] = jnp.where(in_low, near_now, extra_now)
+        for at in range(3):
+            span = slice(at * rows, (at + 1) * rows)
+            mine, other = own_stat[head, at : at + 1, :], near_stat[head, at : at + 1, :]
+            to_left[head, :, span] = jnp.where(in_low, mine, other)
+            to_right[head, :, span] = jnp.where(in_low, other, mine)
 
         @pl.when(has_left)
         def _():
@@ -370,58 +386,99 @@
         def _():
             stat_to_right(head).start()
 
-    def merge(mine, other):
-        top = jnp.maximum(mine[0:1], other[0:1])
-        a = jnp.exp2((mine[0:1] - top) * LOG_SCALE)
-        b = jnp.exp2((other[0:1] - top) * LOG_SCALE)
-        inverse = 1.0 / (mine[1:2] * a + other[1:2] * b)
-        return a * inverse, (mine[2:3] * a + other[2:3] * b) * inverse
-
-    def backward_terms(e_ref, p_ref, mine, other, queries, grads):
-        weight, delta = merge(mine, other)
+        def swapped(block):
+            return jnp.concatenate([block[:, tile:], block[:, :tile]], axis=1)
+
+        @pl.when(jnp.logical_not(has_left))
+        def _():
+            for at in range(3):
+                span = slice(at * rows, (at + 1) * rows)
+                from_left[head, :, span] = swapped(to_left[head, :, span])
+
+        @pl.when(jnp.logical_not(has_right))
+        def _():
+            for at in range(3):
+                span = slice(at * rows, (at + 1) * rows)
+                from_right[head, :, span] = swapped(to_right[head, :, span])
+
+    def merge(stat, low_from, high_from):
+        mine = [stat[at : at + 1] for at in range(3)]
+        other = [
+            jnp.where(
+                in_low,
+                low_from[:, at * rows : (at + 1) * rows],
+                high_from[:, at * rows : (at + 1) * rows],
+            )
+            for at in range(3)
+        ]
+        top = jnp.maximum(mine[0], other[0])
+        a = jnp.exp2((mine[0] - top) * LOG_SCALE)
+        b = jnp.exp2((other[0] - top) * LOG_SCALE)
+        inverse = 1.0 / (mine[1] * a + other[1] * b)
+        return a * inverse, (mine[2] * a + other[2] * b) * inverse
+
+    def backward_terms(e_ref, p_ref, weight, delta, queries, grads):
         probs = e_ref[...] * weight
         dscores = (probs * (p_ref[...] - delta)).astype(jnp.bfloat16)
         return dot(dscores, queries, NN), dot(probs.astype(jnp.bfloat16), grads, NN)
 
     def backward(head):
         slot = head % (LAG + 1)
+        part = head % (FINISH_LAG + 1)
         left_stat, right_stat = from_left[head], from_right[head]
-        from_low = jnp.logical_and(jnp.logical_or(in_low, me == space - 1), me > 0)
-        other = jnp.where(from_low, left_stat[8:16], right_stat[8:16])
         dkey, dvalue = backward_terms(
-            e_own.at[slot], p_own.at[slot], own_stat[head], other, own[head, 0], own[head, 1]
-        )
-        other = jnp.where(in_low, right_stat[0:8], left_stat[0:8])
+            e_own.at[slot],
+            p_own.at[slot],
+            *merge(own_stat[head], left_stat, right_stat),
+            own[head, 0],
+            own[head, 1],
+        )
         near_dkey, near_dvalue = backward_terms(
-            e_near.at[slot], p_near.at[slot], near_stat[head], other, near[head, 0], near[head, 1]
-        )
-        dk[head, low, :] = dkey[:tile] + near_dkey[:, :HS]
-        dk[head, high, :] = dkey[tile:] + near_dkey[:, HS:]
-        dv[low, :] = dvalue[:tile] + near_dvalue[:, :HS]
-        dv[high, :] = dvalue[tile:] + near_dvalue[:, HS:]
-
-    def backward_extra(head):
-        slot = head % (LAG + 1)
-        other = jnp.where(in_low, from_left[head, 0:8, :], from_right[head, 0:8, :])
-        dkey, dvalue = backward_terms(
-            e_extra.at[slot],
-            p_extra.at[slot],
-            extra_stat[head],
-            other,
-            extra[head, 0],
-            extra[head, 1],
-        )
-        dk[head, low, :] += dkey[:, :HS]
-        dk[head, high, :] += dkey[:, HS:]
-        dv[low, :] += dvalue[:, :HS]
-        dv[high, :] += dvalue[:, HS:]
+            e_near.at[slot],
+            p_near.at[slot],
+            *merge(near_stat[head], right_stat, left_stat),
+            near[head, 0],
+            near[head, 1],
+        )
+        for total, mine, terms, at in (
+            (dk.at[head], dkey, near_dkey, first),
+            (dv.at[part], dvalue, near_dvalue, second),
+        ):
+            total[low, :] = mine[:tile] + jnp.where(has_left, terms[:, :HS], 0.0)
+            total[high, :] = mine[tile:] + jnp.where(has_right, terms[:, HS:], 0.0)
+            edge_out[head, :, at] = jnp.where(has_left, terms[:, HS:], terms[:, :HS]).astype(
+                jnp.bfloat16
+            )
+
+    def send_edge(head):
+        @pl.when(jnp.logical_not(has_left))
+        def _():
+            edge_copy(head, right).start()
+
+        @pl.when(jnp.logical_not(has_right))
+        def _():
+            edge_copy(head, left).start()
+
+    def add_edge(head):
+        part = head % (FINISH_LAG + 1)
+
+        @pl.when(beside_first)
+        def _():
+            edge_copy(head, right).wait_recv()
+            dk[head, low, :] += edge_in[head, :, first].astype(jnp.float32)
+            dv[part, low, :] += edge_in[head, :, second].astype(jnp.float32)
+
+        @pl.when(beside_last)
+        def _():
+            edge_copy(head, left).wait_recv()
+            dk[head, high, :] += edge_in[head, :, first].astype(jnp.float32)
+            dv[part, high, :] += edge_in[head, :, second].astype(jnp.float32)
 
     def store_v(head):
         return pltpu.make_async_copy(v_grad.at[head], v_out.at[:, columns(head)], v_sem.at[head])
 
     def finish(head):
-        v_grad[head] = dv[...].astype(jnp.bfloat16)
-        store_v(head).start()
+        v_grad[head] = dv[head % (FINISH_LAG + 1)].astype(jnp.bfloat16)
         total = dk[head] * SCALE
         kn = k_raw[:, columns(head)].astype(jnp.float32) * k_inv[...]
         gain_part[pl.ds(head, 1), :] = jnp.sum(total * kn, axis=0, keepdims=True)
@@ -438,13 +495,15 @@
         def _():
             near_to_left(head).wait_recv()
 
-        @pl.when(extra_left)
-        def _():
-            extra_to_right(head).wait_recv()
-
-        @pl.when(extra_right)
-        def _():
-            extra_to_left(head).wait_recv()
+        @pl.when(jnp.logical_not(has_left))
+        def _():
+            for copy in keys_to_first(head):
+                copy.wait_recv()
+
+        @pl.when(jnp.logical_not(has_right))
+        def _():
+            for copy in keys_to_last(head):
+                copy.wait_recv()
 
     def wait_stat(head):
         @pl.when(has_left)
@@ -455,43 +514,32 @@
         def _():
             stat_to_left(head).wait_recv()
 
-    @pl.loop(0, LAG)
-    def _(head):
-        wait_near(head)
-        forward(head)
-
-        @pl.when(is_extra)
-        def _():
-            forward_extra(head)
-
-        tell(head)
-
-    @pl.loop(LAG, heads)
-    def _(head):
-        behind = head - LAG
-        wait_near(head)
-        wait_stat(behind)
-        forward(head)
-        backward(behind)
-
-        @pl.when(is_extra)
-        def _():
-            forward_extra(head)
-            backward_extra(behind)
-
-        tell(head)
-        finish(behind)
-
-    @pl.loop(heads - LAG, heads)
-    def _(head):
-        wait_stat(head)
-        backward(head)
-
-        @pl.when(is_extra)
-        def _():
-            backward_extra(head)
-
-        finish(head)
+    last_backward = heads + LAG
+    last_finish = last_backward + FINISH_LAG
+    cuts = sorted({0, LAG, LAG + FINISH_LAG, heads - LEAD, heads, last_backward, last_finish})
+    for begin, end in zip(cuts, cuts[1:]):
+
+        @pl.loop(begin, end)
+        def _(step):
+            ahead, behind, ending = step, step - LAG, step - LAG - FINISH_LAG
+            goes_forward = begin < heads
+            goes_back = LAG <= begin < last_backward
+            finishes = begin >= LAG + FINISH_LAG
+            if goes_forward:
+                wait_near(ahead)
+            if begin < heads - LEAD:
+                send_near(step + LEAD)
+            if goes_forward:
+                forward(ahead)
+                tell(ahead)
+            if goes_back:
+                wait_stat(behind)
+                backward(behind)
+                send_edge(behind)
+            if finishes:
+                add_edge(ending)
+                finish(ending)
+                store_v(ending).start()
 
     mean = jnp.sum(row_dot[...], axis=-1, keepdims=True) * (1.0 / features)
     row_dot[...] = jnp.broadcast_to(mean, row_dot.shape)
@@ -549,13 +597,11 @@
             copy.wait_send()
 
     result = total[:heads] * factor
-    k_gain_out[...] = result
-    q_gain_out[...] = result
     for head in range(heads):
         cut = slice(head * HS, (head + 1) * HS)
-        q_gain_out[head : head + 1, :] = (
-            result[head : head + 1] * k_gain[:, cut] / q_gain[:, cut]
-        )
+        row = result[head : head + 1]
+        k_gain_out[cut] = row.reshape(HS)
+        q_gain_out[cut] = (row * k_gain[:, cut] / q_gain[:, cut]).reshape(HS)
 
     @pl.loop(0, heads)
     def _(head):
@@ -571,13 +617,23 @@
             near_to_left(head).wait_send()
             stat_to_left(head).wait_send()
 
+        @pl.when(beside_first)
+        def _():
+            for copy in keys_to_first(head):
+                copy.wait_send()
+
+        @pl.when(beside_last)
+        def _():
+            for copy in keys_to_last(head):
+                copy.wait_send()
+
         @pl.when(jnp.logical_not(has_left))
         def _():
-            extra_to_right(head).wait_send()
+            edge_copy(head, right).wait_send()
 
         @pl.when(jnp.logical_not(has_right))
         def _():
-            extra_to_left(head).wait_send()
+            edge_copy(head, left).wait_send()
 
     for head in range(heads):
         store_k(head).wait()
@@ -601,8 +657,8 @@
         out_shape=(
             jax.ShapeDtypeStruct((rows, features), bf16),
             jax.ShapeDtypeStruct((rows, features), bf16),
-            jax.ShapeDtypeStruct((heads, HS), f32),
-            jax.ShapeDtypeStruct((heads, HS), f32),
+            jax.ShapeDtypeStruct((features,), f32),
+            jax.ShapeDtypeStruct((features,), f32),
         ),
         in_specs=[hbm] * 4 + [vmem] * 2,
         out_specs=(hbm, hbm, vmem, vmem),
@@ -614,32 +670,35 @@
             pltpu.VMEM((heads, rows, HS), bf16),
             pltpu.VMEM((rows, HS), f32),
             pltpu.VMEM((heads, 2, rows, 2 * HS), bf16),
-            pltpu.VMEM((heads, 2, rows, 2 * HS), bf16),
+            pltpu.VMEM((heads, 2, tile, HS), bf16),
             pltpu.VMEM((slots, rows, rows), f32),
             pltpu.VMEM((slots, rows, rows), f32),
             pltpu.VMEM((slots, tile, rows), f32),
             pltpu.VMEM((slots, tile, rows), f32),
-            pltpu.VMEM((slots, tile, rows), f32),
-            pltpu.VMEM((slots, tile, rows), f32),
             pltpu.VMEM((heads, rows, HS), f32),
-            pltpu.VMEM((rows, HS), f32),
+            pltpu.VMEM((FINISH_LAG + 1, rows, HS), f32),
             pltpu.VMEM((heads, rows, HS), bf16),
             pltpu.VMEM((rows, HS), f32),
             pltpu.VMEM((heads, 8, rows), f32),
             pltpu.VMEM((heads, 8, rows), f32),
-            pltpu.VMEM((heads, 8, rows), f32),
-            pltpu.VMEM((heads, 16, rows), f32),
-            pltpu.VMEM((heads, 16, rows), f32),
-            pltpu.VMEM((heads, 16, rows), f32),
-            pltpu.VMEM((heads, 16, rows), f32),
+            pltpu.VMEM((heads, 1, 3 * rows), f32),
+            pltpu.VMEM((heads, 1, 3 * rows), f32),
+            pltpu.VMEM((heads, 1, 3 * rows), f32),
+            pltpu.VMEM((heads, 1, 3 * rows), f32),
+            pltpu.VMEM((heads, tile, 2 * HS), bf16),
+            pltpu.VMEM((heads, tile, 2 * HS), bf16),
             pltpu.VMEM((padded, HS), f32),
             pltpu.VMEM((len(stages), 4, padded, HS), f32),
+            pltpu.VMEM((1, features), f32),
+            pltpu.VMEM((1, features), f32),
             dma((3,)),
             dma((heads,)),
             dma((2, heads)),
             dma((2, heads)),
             dma((2, heads)),
             dma((2, heads)),
+            dma((heads,)),
+            dma((heads,)),
             dma((2, heads)),
             dma((2, heads)),
             dma((heads,)),
@@ -655,10 +714,10 @@
         keys_raw[0],
         values[0],
         out_grad[0],
-        q_gain.reshape(1, features),
-        k_gain.reshape(1, features),
+        q_gain,
+        k_gain,
     )
-    return key_grad[None], value_grad[None], q_sum.reshape(features), k_sum.reshape(features)
+    return key_grad[None], value_grad[None], q_sum, k_sum
 
 
 def solution(mesh):

time: 89 us -> 65.1 us (0.73)
  Pallas kernels: 79.4 us -> 57.8 us
  local copies, waits for them, and re-layouts: 8.2 us -> 5.57 us
    pallas_call x1, Pallas kernels: 79.4 us -> 57.8 us  [per_device(): pl.pallas_call(functools.partial(kernel, stages, space, factor), out_shap...]
    reshape x2 -> x0, local copies, waits for them, and re-layouts: 2.63 us -> none  [the longest x1 1.31 us: per_device(): q_gain.reshape(1, features)]
where the time goes in v2:
time: 65.1 us; the launch traced here: 64 us
  Pallas kernels  57.8 us (89%)
  local copies, waits for them, and re-layouts  5.57 us (9%)
    pallas_call x1, Pallas kernels, per_device(): pl.pallas_call(functools.partial(kernel, stages, space, factor), out_shap...  57.8 us
    unnamed x10, local copies, waits for them, and re-layouts  5.57 us

profile of v2, /device:TPU:1, one launch (start us, length us, event | category | flops | bytes accessed | tf_op | source)
XLA Modules:
  0.0 64.0 jit_solution(16647202900499385474)
XLA Ops:
  0.6 57.8 %shard_map.93 = (bf16[384,2560]{1,0:T(8,128)(2,1)}, bf16[384,2560]{1,0:T(8,128)(2,1)}, f32[2560]{0:T(1024)}, f32[2560]{0:T(1024)}) custom-call(bf16[384,2560]{1,0:T(8,128)(2,1)} %bitcast.6, bf16[384,2560]{1,0:T(8,128)(2,1)} %bitcast.7, bf16[384,2560]{1,0:T(8,128)(2,1)} %bitcast.8, bf16[384,2560]{1,0:T(8,128)(2,1)} %bitcast.9, f32[2560]{0:T(1024)} %q_gain_flat.1, ...), custom_call_target="tpu_custom_call" | custom-call | tf_op jit(solution)/shard_map/pallas_call | solution.py:655
  58.5 0.0 copy-start
  58.5 3.1 %copy.14 = bf16[1,384,2560]{2,1,0:T(8,128)(2,1)} copy(bf16[1,384,2560]{2,1,0:T(8,128)(2,1)} %bitcast.11) | data formatting | bytes 3932160
  61.6 0.0 copy-done
  61.6 0.0 copy-start.2
  61.6 0.0 copy-start.1
  61.6 1.3 %copy.15 = bf16[1,384,2560]{2,1,0:T(8,128)(2,1)} copy(bf16[1,384,2560]{2,1,0:T(8,128)(2,1)S(1)} %bitcast.10) | data formatting | bytes 3932160
  62.8 0.0 copy-done.2
  62.8 0.6 copy.16
  63.4 0.0 copy-done.1
  63.4 0.6 copy.17
Async XLA Ops:
  58.5 3.1 %copy-start = (bf16[384,2560]{1,0:T(8,128)(2,1)S(1)}, bf16[384,2560]{1,0:T(8,128)(2,1)}, u32[]{:S(2)}) copy-start(bf16[384,2560]{1,0:T(8,128)(2,1)} %get-tuple-element.9) | copy-start | bytes 5898244
  61.6 1.3 %copy-start.2 = (f32[2560]{0:T(1024)S(1)}, f32[2560]{0:T(1024)}, u32[]{:S(2)}) copy-start(f32[2560]{0:T(1024)} %get-tuple-element.18) | copy-start | bytes 30724
  61.6 1.9 %copy-start.1 = (f32[2560]{0:T(1024)S(1)}, f32[2560]{0:T(1024)}, u32[]{:S(2)}) copy-start(f32[2560]{0:T(1024)} %get-tuple-element.19) | copy-start | bytes 30724

commit v3 on v2

--- a/solution.py
+++ b/solution.py
@@ -12,9 +12,11 @@
 EPS = 1e-06
 SCALE = HS ** (-0.5)
 LOG_SCALE = SCALE * math.log2(math.e)
-LAG = 4
+GROUP = 1
+LAG = 6
 FINISH_LAG = 2
-LEAD = 5
+LEAD = 6
+PIECES = 4
 CHUNK = 32
 MESH = pl.DeviceIdType.MESH
 NT = (((1,), (1,)), ((), ()))
@@ -26,13 +28,11 @@
 
 
 def sum_stages(dp, space):
-    def pairs(axis, bits):
-        return [(axis, tuple(bits[i : i + 2])) for i in range(0, len(bits), 2)]
-
-    space_bits = list(range(space.bit_length() - 1))
-    if len(space_bits) == 4:
-        space_bits = [0, 3, 1, 2]
-    return pairs("space", space_bits) + pairs("dp", list(range(dp.bit_length() - 1)))
+    return [
+        (axis, tuple(range(size.bit_length() - 1)))
+        for axis, size in (("space", space), ("dp", dp))
+        if size > 1
+    ]
 
 
 def group_place(index, bits):
@@ -74,7 +74,6 @@
     p_near,
     dk,
     dv,
-    v_grad,
     row_dot,
     own_stat,
     near_stat,
@@ -98,8 +97,6 @@
     edge_recv,
     stat_send,
     stat_recv,
-    v_sem,
-    k_sem,
     gain_send,
     gain_recv,
 ):
@@ -258,14 +255,16 @@
             device_id_type=MESH,
         )
 
-    def send_near(head):
+    def send_near(group):
         @pl.when(has_right)
         def _():
-            near_to_right(head).start()
+            for head in group:
+                near_to_right(head).start()
 
         @pl.when(has_left)
         def _():
-            near_to_left(head).start()
+            for head in group:
+                near_to_left(head).start()
 
     @pl.loop(0, heads)
     def _(head):
@@ -273,7 +272,7 @@
 
     @pl.loop(0, LEAD)
     def _(head):
-        send_near(head)
+        send_near([head])
 
     @pl.loop(0, heads)
     def _(head):
@@ -357,7 +356,7 @@
             ref[slot, at : at + 1, :] = row
 
     def forward(head):
-        slot = head % (LAG + 1)
+        slot = head % ((LAG + 1) * GROUP)
         keys, values = key[head], value[:, columns(head)]
         stat = scores(keys, values, own[head, 0], own[head, 1], e_own.at[slot], p_own.at[slot])
         put_stat(own_stat, head, stat)
@@ -371,35 +370,37 @@
         )
         put_stat(near_stat, head, stat)
 
-    def tell(head):
-        for at in range(3):
-            span = slice(at * rows, (at + 1) * rows)
-            mine, other = own_stat[head, at : at + 1, :], near_stat[head, at : at + 1, :]
-            to_left[head, :, span] = jnp.where(in_low, mine, other)
-            to_right[head, :, span] = jnp.where(in_low, other, mine)
-
-        @pl.when(has_left)
-        def _():
-            stat_to_left(head).start()
-
-        @pl.when(has_right)
-        def _():
-            stat_to_right(head).start()
-
-        def swapped(block):
-            return jnp.concatenate([block[:, tile:], block[:, :tile]], axis=1)
-
-        @pl.when(jnp.logical_not(has_left))
-        def _():
+    def tell(group):
+        for head in group:
             for at in range(3):
                 span = slice(at * rows, (at + 1) * rows)
-                from_left[head, :, span] = swapped(to_left[head, :, span])
+                mine, other = own_stat[head, at : at + 1, :], near_stat[head, at : at + 1, :]
+                to_left[head, :, span] = jnp.where(in_low, mine, other)
+                to_right[head, :, span] = jnp.where(in_low, other, mine)
+
+        def swap(source, target):
+            for head in group:
+                for at in range(0, 3 * rows, rows):
+                    target[head, :, at : at + tile] = source[head, :, at + tile : at + rows]
+                    target[head, :, at + tile : at + rows] = source[head, :, at : at + tile]
+
+        @pl.when(has_left)
+        def _():
+            for head in group:
+                stat_to_left(head).start()
+
+        @pl.when(has_right)
+        def _():
+            for head in group:
+                stat_to_right(head).start()
+
+        @pl.when(jnp.logical_not(has_left))
+        def _():
+            swap(to_left, from_left)
 
         @pl.when(jnp.logical_not(has_right))
         def _():
-            for at in range(3):
-                span = slice(at * rows, (at + 1) * rows)
-                from_right[head, :, span] = swapped(to_right[head, :, span])
+            swap(to_right, from_right)
 
     def merge(stat, low_from, high_from):
         mine = [stat[at : at + 1] for at in range(3)]
@@ -423,8 +424,8 @@
         return dot(dscores, queries, NN), dot(probs.astype(jnp.bfloat16), grads, NN)
 
     def backward(head):
-        slot = head % (LAG + 1)
-        part = head % (FINISH_LAG + 1)
+        slot = head % ((LAG + 1) * GROUP)
+        part = head % ((FINISH_LAG + 1) * GROUP)
         left_stat, right_stat = from_left[head], from_right[head]
         dkey, dvalue = backward_terms(
             e_own.at[slot],
@@ -450,35 +451,35 @@
                 jnp.bfloat16
             )
 
-    def send_edge(head):
+    def send_edge(group):
         @pl.when(jnp.logical_not(has_left))
         def _():
-            edge_copy(head, right).start()
+            for head in group:
+                edge_copy(head, right).start()
 
         @pl.when(jnp.logical_not(has_right))
         def _():
-            edge_copy(head, left).start()
-
-    def add_edge(head):
-        part = head % (FINISH_LAG + 1)
+            for head in group:
+                edge_copy(head, left).start()
+
+    def add_edge(group):
+        def add(span):
+            for head in group:
+                part = head % ((FINISH_LAG + 1) * GROUP)
+                edge_copy(head, left).wait_recv()
+                dk[head, span, :] += edge_in[head, :, first].astype(jnp.float32)
+                dv[part, span, :] += edge_in[head, :, second].astype(jnp.float32)
 
         @pl.when(beside_first)
         def _():
-            edge_copy(head, right).wait_recv()
-            dk[head, low, :] += edge_in[head, :, first].astype(jnp.float32)
-            dv[part, low, :] += edge_in[head, :, second].astype(jnp.float32)
+            add(low)
 
         @pl.when(beside_last)
         def _():
-            edge_copy(head, left).wait_recv()
-            dk[head, high, :] += edge_in[head, :, first].astype(jnp.float32)
-            dv[part, high, :] += edge_in[head, :, second].astype(jnp.float32)
-
-    def store_v(head):
-        return pltpu.make_async_copy(v_grad.at[head], v_out.at[:, columns(head)], v_sem.at[head])
+            add(high)
 
     def finish(head):
-        v_grad[head] = dv[head % (FINISH_LAG + 1)].astype(jnp.bfloat16)
+        v_out[:, columns(head)] = dv[head % ((FINISH_LAG + 1) * GROUP)].astype(jnp.bfloat16)
         total = dk[head] * SCALE
         kn = k_raw[:, columns(head)].astype(jnp.float32) * k_inv[...]
         gain_part[pl.ds(head, 1), :] = jnp.sum(total * kn, axis=0, keepdims=True)
@@ -486,76 +487,81 @@
         dk[head] = dkn
         row_dot[...] += dkn * kn
 
-    def wait_near(head):
+    def wait_near(group):
         @pl.when(has_left)
         def _():
-            near_to_right(head).wait_recv()
+            for head in group:
+                near_to_right(head).wait_recv()
 
         @pl.when(has_right)
         def _():
-            near_to_left(head).wait_recv()
+            for head in group:
+                near_to_left(head).wait_recv()
 
         @pl.when(jnp.logical_not(has_left))
         def _():
-            for copy in keys_to_first(head):
-                copy.wait_recv()
+            for head in group:
+                for copy in keys_to_first(head):
+                    copy.wait_recv()
 
         @pl.when(jnp.logical_not(has_right))
         def _():
-            for copy in keys_to_last(head):
-                copy.wait_recv()
-
-    def wait_stat(head):
+            for head in group:
+                for copy in keys_to_last(head):
+                    copy.wait_recv()
+
+    def wait_stat(group):
         @pl.when(has_left)
         def _():
-            stat_to_right(head).wait_recv()
+            for head in group:
+                stat_to_right(head).wait_recv()
 
         @pl.when(has_right)
         def _():
-            stat_to_left(head).wait_recv()
-
-    last_backward = heads + LAG
+            for head in group:
+                stat_to_left(head).wait_recv()
+
+    groups = heads // GROUP
+    last_backward = groups + LAG
     last_finish = last_backward + FINISH_LAG
-    cuts = sorted({0, LAG, LAG + FINISH_LAG, heads - LEAD, heads, last_backward, last_finish})
+    last_send = groups - LEAD // GROUP
+    cuts = sorted({0, LAG, LAG + FINISH_LAG, last_send, groups, last_backward, last_finish})
     for begin, end in zip(cuts, cuts[1:]):
 
         @pl.loop(begin, end)
         def _(step):
-            ahead, behind, ending = step, step - LAG, step - LAG - FINISH_LAG
-            goes_forward = begin < heads
+            ahead, behind, ending = [
+                [(step - late) * GROUP + at for at in range(GROUP)]
+                for late in (0, LAG, LAG + FINISH_LAG)
+            ]
+            if begin < groups:
+                wait_near(ahead)
+                if begin < last_send:
+                    send_near([head + LEAD for head in ahead])
+                for head in ahead:
+                    forward(head)
+                tell(ahead)
             goes_back = LAG <= begin < last_backward
             finishes = begin >= LAG + FINISH_LAG
-            if goes_forward:
-                wait_near(ahead)
-            if begin < heads - LEAD:
-                send_near(step + LEAD)
-            if goes_forward:
-                forward(ahead)
-                tell(ahead)
             if goes_back:
                 wait_stat(behind)
-                backward(behind)
-                send_edge(behind)
             if finishes:
                 add_edge(ending)
-                finish(ending)
-                store_v(ending).start()
+                for head in ending:
+                    finish(head)
+            if goes_back:
+                for head in behind:
+                    backward(head)
+                send_edge(behind)
 
     mean = jnp.sum(row_dot[...], axis=-1, keepdims=True) * (1.0 / features)
     row_dot[...] = jnp.broadcast_to(mean, row_dot.shape)
 
-    def store_k(head):
-        columns_now = slice(head * HS, (head + 1) * HS)
-        return pltpu.make_async_copy(
-            q_raw.at[:, columns_now], k_out.at[:, columns_now], k_sem.at[head]
-        )
-
     def key_pass(head):
         kn = k_raw[:, head * HS : (head + 1) * HS].astype(jnp.float32) * k_inv[...]
-        q_raw[:, head * HS : (head + 1) * HS] = (
+        k_out[:, head * HS : (head + 1) * HS] = (
             k_inv[...] * (dk[head] - kn * row_dot[...])
         ).astype(jnp.bfloat16)
-        store_k(head).start()
 
     total = gain_part[...]
     done = 0
@@ -596,7 +602,7 @@
         for copy in copies:
             copy.wait_send()
 
-    result = total[:heads] * factor
+    result = total * factor
     for head in range(heads):
         cut = slice(head * HS, (head + 1) * HS)
         row = result[head : head + 1]
@@ -605,8 +611,6 @@
 
     @pl.loop(0, heads)
     def _(head):
-        store_v(head).wait()
-
         @pl.when(has_right)
         def _():
             near_to_right(head).wait_send()
@@ -635,8 +639,23 @@
         def _():
             edge_copy(head, left).wait_send()
 
-    for head in range(heads):
-        store_k(head).wait()
+
+def hand_over(key_now, value_now, q_now, k_now, key_out, value_out, q_out, k_out, sem):
+    rows = key_now.shape[0] // PIECES
+    copies = [
+        pltpu.make_async_copy(q_now, q_out, sem.at[2, 0]),
+        pltpu.make_async_copy(k_now, k_out, sem.at[2, 1]),
+    ]
+    for at, (source, target) in enumerate(((key_now, key_out), (value_now, value_out))):
+        for piece in range(PIECES):
+            span = pl.ds(piece * rows, rows)
+            copies.append(
+                pltpu.make_async_copy(source.at[span], target.at[span], sem.at[at, piece])
+            )
+    for copy in copies:
+        copy.start()
+    for copy in copies:
+        copy.wait()
 
 
 def per_device(queries_raw, keys_raw, values, out_grad, q_gain, k_gain):
@@ -646,22 +665,22 @@
     dp, space = lax.axis_size("dp"), lax.axis_size("space")
     stages = sum_stages(dp, space)
     factor = (dp * space * rows) ** (-0.5)
-    slots = LAG + 1
+    slots = (LAG + 1) * GROUP
     bf16, f32 = jnp.bfloat16, jnp.float32
-    padded = (heads + 7) // 8 * 8
+    most = max(dp, space)
     hbm = pl.BlockSpec(memory_space=pl.ANY)
     vmem = pl.BlockSpec(memory_space=pltpu.VMEM)
     dma = pltpu.SemaphoreType.DMA
     key_grad, value_grad, q_sum, k_sum = pl.pallas_call(
         functools.partial(kernel, stages, space, factor),
         out_shape=(
-            jax.ShapeDtypeStruct((rows, features), bf16),
-            jax.ShapeDtypeStruct((rows, features), bf16),
-            jax.ShapeDtypeStruct((features,), f32),
-            jax.ShapeDtypeStruct((features,), f32),
+            pltpu.VMEM((rows, features), bf16),
+            pltpu.VMEM((rows, features), bf16),
+            pltpu.VMEM((features,), f32),
+            pltpu.VMEM((features,), f32),
         ),
         in_specs=[hbm] * 4 + [vmem] * 2,
-        out_specs=(hbm, hbm, vmem, vmem),
+        out_specs=(vmem,) * 4,
         scratch_shapes=[
             pltpu.VMEM((rows, features), bf16),
             pltpu.VMEM((rows, features), bf16),
@@ -676,8 +695,7 @@
             pltpu.VMEM((slots, tile, rows), f32),
             pltpu.VMEM((slots, tile, rows), f32),
             pltpu.VMEM((heads, rows, HS), f32),
-            pltpu.VMEM((FINISH_LAG + 1, rows, HS), f32),
-            pltpu.VMEM((heads, rows, HS), bf16),
+            pltpu.VMEM(((FINISH_LAG + 1) * GROUP, rows, HS), f32),
             pltpu.VMEM((rows, HS), f32),
             pltpu.VMEM((heads, 8, rows), f32),
             pltpu.VMEM((heads, 8, rows), f32),
@@ -687,8 +705,8 @@
             pltpu.VMEM((heads, 1, 3 * rows), f32),
             pltpu.VMEM((heads, tile, 2 * HS), bf16),
             pltpu.VMEM((heads, tile, 2 * HS), bf16),
-            pltpu.VMEM((padded, HS), f32),
-            pltpu.VMEM((len(stages), 4, padded, HS), f32),
+            pltpu.VMEM((heads, HS), f32),
+            pltpu.VMEM((len(stages), most, heads, HS), f32),
             pltpu.VMEM((1, features), f32),
             pltpu.VMEM((1, features), f32),
             dma((3,)),
@@ -701,13 +719,11 @@
             dma((heads,)),
             dma((2, heads)),
             dma((2, heads)),
-            dma((heads,)),
-            dma((heads,)),
-            dma((len(stages), 4)),
-            dma((len(stages), 4)),
+            dma((len(stages), most)),
+            dma((len(stages), most)),
         ],
         compiler_params=pltpu.CompilerParams(
-            collective_id=0, has_side_effects=True, vmem_limit_bytes=60 * 2**20
+            collective_id=0, has_side_effects=True, vmem_limit_bytes=54 * 2**20
         ),
     )(
         queries_raw[0],
@@ -717,6 +733,15 @@
         q_gain,
         k_gain,
     )
+    results = (key_grad, value_grad, q_sum, k_sum)
+    key_grad, value_grad, q_sum, k_sum = pl.pallas_call(
+        hand_over,
+        out_shape=tuple(jax.ShapeDtypeStruct(result.shape, result.dtype) for result in results),
+        in_specs=[hbm] * 4,
+        out_specs=(hbm,) * 4,
+        scratch_shapes=[dma((3, PIECES))],
+        compiler_params=pltpu.CompilerParams(vmem_limit_bytes=2**20),
+    )(*[pltpu.with_memory_space_constraint(result, pltpu.VMEM) for result in results])
     return key_grad[None], value_grad[None], q_sum, k_sum
 
 

time: 65.1 us -> 57.7 us (0.89)
  local copies, waits for them, and re-layouts: 5.57 us -> 0 us
  Pallas kernels: 57.8 us -> 56.4 us
    unnamed x10 -> x0, local copies, waits for them, and re-layouts: 5.57 us -> none
    pallas_call x1, Pallas kernels: 57.8 us -> 54.3 us  [per_device(): pl.pallas_call(functools.partial(kernel, stages, space, factor), out_shap...]
    pallas_call x0 -> x1, Pallas kernels: none -> 2.03 us  [per_device(): pl.pallas_call(hand_over, out_shape=tuple((jax.ShapeDtypeStruct(result.sh...]
where the time goes in v3:
time: 57.7 us; the launch traced here: 57 us
  Pallas kernels  56.4 us (98%)
  between operations  0.64 us (1%)
    pallas_call x1, Pallas kernels, per_device(): pl.pallas_call(functools.partial(kernel, stages, space, factor), out_shap...  54.3 us
    pallas_call x1, Pallas kernels, per_device(): pl.pallas_call(hand_over, out_shape=tuple((jax.ShapeDtypeStruct(result.sh...  2.03 us

profile of v3, /device:TPU:1, one launch (start us, length us, event | category | flops | bytes accessed | tf_op | source)
XLA Modules:
  0.0 57.0 jit_solution(17550646632618665102)
XLA Ops:
  0.6 54.3 %shard_map.93 = (bf16[384,2560]{1,0:T(8,128)(2,1)S(1)}, bf16[384,2560]{1,0:T(8,128)(2,1)S(1)}, f32[2560]{0:T(1024)S(1)}, f32[2560]{0:T(1024)S(1)}) custom-call(bf16[384,2560]{1,0:T(8,128)(2,1)} %bitcast.6, bf16[384,2560]{1,0:T(8,128)(2,1)} %bitcast.7, bf16[384,2560]{1,0:T(8,128)(2,1)} %bitcast.8, bf16[384,2560]{1,0:T(8,128)(2,1)} %bitcast.9, ...), custom_call_target="tpu_custom_call" | custom-call | tf_op jit(solution)/shard_map/pallas_call | solution.py:674
  55.0 2.0 %shard_map.94 = (bf16[384,2560]{1,0:T(8,128)(2,1)}, bf16[384,2560]{1,0:T(8,128)(2,1)}, f32[2560]{0:T(1024)}, f32[2560]{0:T(1024)}) custom-call(bf16[384,2560]{1,0:T(8,128)(2,1)S(1)} %get-tuple-element.12.key_now, bf16[384,2560]{1,0:T(8,128)(2,1)S(1)} %get-tuple-element.13.value_now, f32[2560]{0:T(1024)S(1)} %get-tuple-element.14.q_now, ...), custom_call_target="tpu_custom_call" | custom-call | tf_op jit(solution)/shard_map/pallas_call | solution.py:737
